TPU v7x, 256 devices: a whole 4x4x8 slice. The times are simulated.
256 devices in a mesh: pool: 32 (over x, z_lo, y), tensor: 8 (over z_hi, core).
Axes of the slice: x: 4, y: 4, z: 8 (z_hi: 4, z_lo: 2; z = z_hi * 2 + z_lo), core: 2. Of those that a mesh axis runs over, the one named last changes fastest.
Arguments:
- queries: bfloat16 [16384, 4096], P('pool', 'tensor'), may hold values from -400 to 400
- new_key_value: bfloat16 [16384, 2, 1024], P('pool', None, 'tensor'), may hold values from -5 to 5
- saved_key_value: bfloat16 [1024, 128, 2, 1024], P('pool', None, None, 'tensor'), may hold values from -5 to 5
- out_weight: bfloat16 [4096, 5120], P('tensor'), may hold values from -5 to 5
- hist_owner: int32 [32, 64], P('pool'), may hold values from 0 to 31, as said below
- hist_block: int32 [32, 64], P('pool'), may hold values from 0 to 31
- hist_len: int32 [32], P('pool'), may hold values from 8 to 64, as said below
- evict: int32 [32], P('pool'), may hold values 0 or 1
- dest_owner: int32 [32, 4], P('pool'), may hold values from 0 to 31, as said below
- dest_slot: int32 [32, 4], P('pool'), may hold values from 0 to 31, as said below
Outputs:
- attn_out: bfloat16 [16384, 5120], P(('pool', 'tensor'))
- pool_out: bfloat16 [1024, 128, 2, 1024], P('pool', None, None, 'tensor')
Inputs may be any that keep to these rules, and one draw needn't show every extreme that they name: `hist_owner`: in row p each owner appears exactly 2 times among all 64 entries, so at most 2 times among the first hist_len[p]. `hist_len`: some instance has all 64 blocks. `dest_owner`: the 4 owners of one row are distinct, and each column names every owner once. All pairs (dest_owner, dest_slot) are distinct.
All inputs are finite; a program needn't handle non-finite values. No bound on the sum of `evict` on one device may be relied on, other than what follows from the above.
Results may differ from a plain program's by a relative error of at most 0.017.
Values may be sent and summed in bfloat16 or wider, within the bound.
No kernel may reach another device: no remote copies, remote signals or barrier semaphores. Data moves between devices by JAX's collectives and lax.ppermute only.
A program may use at most 128 MiB of HBM per device.

v0:
```python
import math

import jax
import jax.numpy as jnp
from jax import lax
from jax.sharding import PartitionSpec as P

HEAD_SIZE = 128


def slot_table(owner_row, block_row, length, pool_size, capacity):
    list_len = owner_row.shape[0]
    live_rows = jnp.arange(list_len, dtype=jnp.int32) < length
    matches = (owner_row[:, None] == jnp.arange(pool_size, dtype=jnp.int32)[None, :]) & live_rows[
        :, None
    ]
    ranking = jnp.cumsum(matches.astype(jnp.int32), axis=0) - 1
    placed = matches[:, :, None] & (
        ranking[:, :, None] == jnp.arange(capacity, dtype=jnp.int32)[None, None, :]
    )
    wanted = jnp.sum(jnp.where(placed, block_row[:, None, None], 0), axis=0)
    return jnp.where(jnp.any(placed, axis=0), wanted, -1)


def on_device(
    queries,
    new_key_value,
    saved_key_value,
    out_weight,
    hist_owner,
    hist_block,
    hist_len,
    evict,
    dest_owner,
    dest_slot,
):
    pool_size = lax.axis_size("pool")
    capacity = hist_owner.shape[1] // pool_size
    new_rows = queries.shape[0]
    kv_width = new_key_value.shape[2]
    block_len = saved_key_value.shape[1]
    head_grouping = queries.shape[1] // kv_width
    pool_ids = jnp.arange(pool_size, dtype=jnp.int32)
    fresh_blocks = new_key_value.reshape(-1, block_len * 2 * kv_width)
    chosen = (dest_owner[0][None, :] == pool_ids[:, None]) & (evict[0] > 0)
    outgoing_blocks = jnp.dot(
        chosen.astype(jnp.bfloat16), fresh_blocks, preferred_element_type=jnp.float32
    ).astype(jnp.bfloat16)
    outgoing_blocks = outgoing_blocks.reshape(pool_size, 1, block_len, 2, kv_width)
    outgoing_slots = jnp.where(
        jnp.any(chosen, axis=1), jnp.sum(jnp.where(chosen, dest_slot[0][None, :], 0), axis=1), -1
    )
    outgoing_slots = outgoing_slots.reshape(pool_size, 1)
    requested = slot_table(hist_owner[0], hist_block[0], hist_len[0], pool_size, capacity)
    fetched = lax.all_to_all(
        saved_key_value[
            jnp.maximum(
                lax.all_to_all(requested, "pool", split_axis=0, concat_axis=0, tiled=True), 0
            )
        ],
        "pool",
        split_axis=0,
        concat_axis=0,
        tiled=True,
    )
    incoming_blocks, incoming_slots = (
        lax.all_to_all(outgoing_blocks, "pool", split_axis=0, concat_axis=0, tiled=True),
        lax.all_to_all(outgoing_slots, "pool", split_axis=0, concat_axis=0, tiled=True),
    )
    saved = fetched.reshape(-1, 2, kv_width)
    key_rows = jnp.concatenate([saved[:, 0], new_key_value[:, 0]], axis=0)
    value_rows = jnp.concatenate([saved[:, 1], new_key_value[:, 1]], axis=0)
    live_keys = jnp.repeat((requested >= 0).reshape(-1), block_len)
    saved_count = live_keys.shape[0]
    score_scale = 1.0 / math.sqrt(HEAD_SIZE)
    row_total = head_grouping * new_rows
    row_block = min(512, row_total)
    token_of_row = (jnp.arange(row_total, dtype=jnp.int32) % new_rows).reshape(-1, row_block)
    new_positions = jnp.arange(new_rows, dtype=jnp.int32)
    head_queries = queries
    head_queries = head_queries.reshape(new_rows, head_grouping, HEAD_SIZE).transpose(1, 0, 2)

    def attend(block_parts):
        query_block, token_block = block_parts
        scores = (
            jnp.einsum("rd,kd->rk", query_block, key_rows, preferred_element_type=jnp.float32)
            * score_scale
        )
        allowed = jnp.concatenate(
            [
                jnp.broadcast_to(live_keys[None, :], (query_block.shape[0], saved_count)),
                new_positions[None, :] <= token_block[:, None],
            ],
            axis=1,
        )
        scores = jnp.where(allowed, scores, -jnp.inf)
        highest = jnp.max(scores, axis=1, keepdims=True)
        weights = jnp.exp(scores - highest)
        normalized = (weights / jnp.sum(weights, axis=1, keepdims=True)).astype(jnp.bfloat16)
        return jnp.dot(normalized, value_rows, preferred_element_type=jnp.float32).astype(
            jnp.bfloat16
        )

    context_head = lax.map(attend, (head_queries, token_of_row))
    contexts = context_head.transpose(1, 0, 2).reshape(new_rows, head_grouping * HEAD_SIZE)
    attn_out = lax.psum_scatter(
        jnp.dot(contexts, out_weight, preferred_element_type=jnp.float32).astype(jnp.bfloat16),
        "tensor",
        scatter_dimension=0,
        tiled=True,
    )
    pool_rows = saved_key_value.shape[0]
    landing = (
        incoming_slots.reshape(1, pool_size) == jnp.arange(pool_rows, dtype=jnp.int32)[:, None]
    )
    written = jnp.dot(
        landing.astype(jnp.bfloat16),
        incoming_blocks.reshape(pool_size, -1),
        preferred_element_type=jnp.float32,
    ).astype(jnp.bfloat16)
    pool_out = jnp.where(
        jnp.any(landing, axis=1)[:, None], written, saved_key_value.reshape(pool_rows, -1)
    ).reshape(saved_key_value.shape)
    return (attn_out, pool_out)


def solution(mesh):
    in_specs = (
        P("pool", "tensor"),
        P("pool", None, "tensor"),
        P("pool", None, None, "tensor"),
        P("tensor", None),
        P("pool", None),
        P("pool", None),
        P("pool"),
        P("pool"),
        P("pool", None),
        P("pool", None),
    )
    out_specs = (P(("pool", "tensor"), None), P("pool", None, None, "tensor"))
    return jax.shard_map(
        on_device, mesh=mesh, in_specs=in_specs, out_specs=out_specs, check_vma=False
    )
```

profile of v0, /device:TPU:4, one launch (start us, length us, event | category | flops | bytes accessed | tf_op | source)
XLA Modules:
  0.0 329.3 jit_solution(7804113498297311398)
XLA Ops:
  7.8 0.7 fusion.12
  8.6 0.1 reduce_window_sum.11
  8.7 0.1 copy.59
  8.7 0.1 copy.58
  8.8 0.1 fusion.14
  9.0 0.8 select_reduce_fusion
  9.7 0.1 copy.60
  9.8 15.0 %all_to_all.22 = s32[32,1,2]{2,1,0:T(1,128)S(1)} all-to-all(s32[32,1,2]{2,1,0:T(1,128)S(1)} %copy.60), channel_id=1, replica_groups=mesh['pool'=32,'tensor'=8] {'pool'}, dimensions={0} | all-to-all | bytes 512 | tf_op jit(solution)/shard_map/all_to_all | solution.py:58
  24.8 0.1 maximum_reduce_fusion
  24.9 0.1 reshape.190
  25.0 12.2 %gather_fusion = bf16[64,128,2,128]{3,2,1,0:T(2,128)(2,1)} fusion(bf16[32,128,2,128]{3,2,1,0:T(2,128)(2,1)} %param.14, s32[1024]{0:T(1024)S(1)} %pad_clamp_fusion), kind=kCustom, calls=%fused_computation | custom fusion | bytes 8388864 | tf_op jit(solution)/shard_map/gather | solution.py:56
  37.2 5.2 %copy.62 = bf16[32,2,128,2,128]{4,2,1,3,0:T(8,128)(2,1)} copy(bf16[32,2,128,2,128]{4,3,2,1,0:T(2,128)(2,1)} %bitcast.58) | data formatting | bytes 8388608 | tf_op jit(solution)/shard_map/gather | solution.py:56
  42.5 7.0 %all-to-all-start.1 = ((bf16[32,2,128,2,128]{4,2,1,3,0:T(8,128)(2,1)}), bf16[32,2,128,2,128]{4,2,1,3,0:T(8,128)(2,1)}, u32[]{:S(2)}, u32[]{:S(2)}) async-start(bf16[32,2,128,2,128]{4,2,1,3,0:T(8,128)(2,1)} %copy.62), calls=%async_computation.1 | async-start | bytes 8388608 | tf_op jit(solution)/shard_map/all_to_all | solution.py:55
  49.5 0.1 copy.66
  49.6 0.1 ge.8
  49.7 0.2 copy.57
  50.0 0.4 fusion.23
  50.4 52.8 %all-to-all-done.1 = bf16[32,2,128,2,128]{4,2,1,3,0:T(8,128)(2,1)} async-done(((bf16[32,2,128,2,128]{4,2,1,3,0:T(8,128)(2,1)}), bf16[32,2,128,2,128]{4,2,1,3,0:T(8,128)(2,1)}, u32[]{:S(2)}, u32[]{:S(2)}) %all-to-all-start.1) | async-done | bytes 4194336 | tf_op jit(solution)/shard_map/all_to_all | solution.py:55
  103.2 2.5 copy.63
  105.7 0.3 slice_bitcast_fusion
  105.9 4.5 %pad_maximum_fusion = bf16[8704,128]{1,0:T(8,128)(2,1)S(1)} fusion(bf16[512,128]{1,0:T(8,128)(2,1)S(1)} %get-tuple-element.121, bf16[8192,128]{1,0:T(8,128)(2,1)S(1)} %get-tuple-element.115), kind=kLoop, calls=%fused_computation.21 | loop fusion | flops 4456448 | bytes 4456448 | tf_op jit(solution)/shard_map/concatenate | solution.py:71
  110.5 5.5 %pad_maximum_fusion.1 = bf16[8704,128]{1,0:T(8,128)(2,1)} fusion(bf16[512,128]{1,0:T(8,128)(2,1)S(1)} %get-tuple-element.120, bf16[8192,128]{1,0:T(8,128)(2,1)S(1)} %get-tuple-element.114), kind=kLoop, calls=%fused_computation.22 | loop fusion | flops 4456448 | bytes 4456448 | tf_op jit(solution)/shard_map/concatenate | solution.py:72
  116.0 108.0 %while.11 = (s32[]{:T(128)}, bf16[4,512,128]{1,2,0:T(8,128)(2,1)S(1)}, s32[4,512]{1,0:T(4,128)S(1)}, bf16[4,512,128]{1,2,0:T(8,128)(2,1)S(1)}, bf16[8704,128]{1,...) while((s32[]{:T(128)}, ...), condition=%wide.region_6.7_spmd.clone, body=%wide.region_3.6_spmd.clone.sunk | while | flops 2322136064 | bytes 59295400 | solution.py:104
  116.0 0.2 iota_compare_fusion.8
  116.2 0.1 broadcast_bitcast_fusion.2
  116.3 8.5 %fusion.37 = (f32[512]{0:T(512)S(1)}, f32[512,8704]{1,0:T(8,128)}) fusion(bf16[8704,128]{1,0:T(8,128)(2,1)S(1)} %get-tuple-element.191, bf16[4,512,128]{1,2,0:T(8,128)(2,1)S(1)} %get-tuple-element.190, s32[]{:T(128)} %get-tuple-element.178, pred[512,512]{1,0:T(32,128)(4,1)S(1)} %iota_compare_fusion.8, pred[8704]{0:T(1024)(128)(4,1)S(1)} %pad.clone.2), kind=kOutput, calls=%fused_computation.52.clone.1 | convolution fusion | flops 1158675968 | bytes 20458500 | tf_op jit(solution)/shard_map/while/body/eval_jaxpr/rd,kd->rk/dot_general | solution.py:86
  124.8 8.5 %fusion.38 = f32[512]{0:T(512)S(1)} fusion(f32[512,8704]{1,0:T(8,128)} %get-tuple-element.167, f32[512]{0:T(512)S(1)} %get-tuple-element.168), kind=kLoop, calls=%fused_computation.6.clone.1 | loop fusion | flops 8912384 | bytes 17829888 | tf_op jit(solution)/shard_map/while/body/eval_jaxpr/reduce_sum | solution.py:99
  133.3 9.5 %fusion.39 = bf16[1,512,128]{2,1,0:T(8,128)(2,1)S(1)} fusion(bf16[8704,128]{1,0:T(8,128)(2,1)} %get-tuple-element.192, f32[512,8704]{1,0:T(8,128)} %get-tuple-element.167, f32[512]{0:T(512)S(1)} %fusion.38, f32[512]{0:T(512)S(1)} %get-tuple-element.168), kind=kOutput, calls=%fused_computation.9.clone.1 | convolution fusion | flops 1154285568 | bytes 20189184 | tf_op jit(solution)/shard_map/while/body/eval_jaxpr/dot_general | solution.py:100
  142.8 0.1 copy.81
  143.0 0.2 iota_compare_fusion.8
  143.2 0.1 broadcast_bitcast_fusion.2
  143.3 8.5 %fusion.37 = (f32[512]{0:T(512)S(1)}, f32[512,8704]{1,0:T(8,128)}) fusion(bf16[8704,128]{1,0:T(8,128)(2,1)S(1)} %get-tuple-element.191, bf16[4,512,128]{1,2,0:T(8,128)(2,1)S(1)} %get-tuple-element.190, s32[]{:T(128)} %get-tuple-element.178, pred[512,512]{1,0:T(32,128)(4,1)S(1)} %iota_compare_fusion.8, pred[8704]{0:T(1024)(128)(4,1)S(1)} %pad.clone.2), kind=kOutput, calls=%fused_computation.52.clone.1 | convolution fusion | flops 1158675968 | bytes 20458500 | tf_op jit(solution)/shard_map/while/body/eval_jaxpr/rd,kd->rk/dot_general | solution.py:86
  151.8 8.5 %fusion.38 = f32[512]{0:T(512)S(1)} fusion(f32[512,8704]{1,0:T(8,128)} %get-tuple-element.167, f32[512]{0:T(512)S(1)} %get-tuple-element.168), kind=kLoop, calls=%fused_computation.6.clone.1 | loop fusion | flops 8912384 | bytes 17829888 | tf_op jit(solution)/shard_map/while/body/eval_jaxpr/reduce_sum | solution.py:99
  160.3 9.5 %fusion.39 = bf16[1,512,128]{2,1,0:T(8,128)(2,1)S(1)} fusion(bf16[8704,128]{1,0:T(8,128)(2,1)} %get-tuple-element.192, f32[512,8704]{1,0:T(8,128)} %get-tuple-element.167, f32[512]{0:T(512)S(1)} %fusion.38, f32[512]{0:T(512)S(1)} %get-tuple-element.168), kind=kOutput, calls=%fused_computation.9.clone.1 | convolution fusion | flops 1154285568 | bytes 20189184 | tf_op jit(solution)/shard_map/while/body/eval_jaxpr/dot_general | solution.py:100
  169.8 0.1 copy.81
  170.0 0.2 iota_compare_fusion.8
  170.2 0.1 broadcast_bitcast_fusion.2
  170.3 8.5 %fusion.37 = (f32[512]{0:T(512)S(1)}, f32[512,8704]{1,0:T(8,128)}) fusion(bf16[8704,128]{1,0:T(8,128)(2,1)S(1)} %get-tuple-element.191, bf16[4,512,128]{1,2,0:T(8,128)(2,1)S(1)} %get-tuple-element.190, s32[]{:T(128)} %get-tuple-element.178, pred[512,512]{1,0:T(32,128)(4,1)S(1)} %iota_compare_fusion.8, pred[8704]{0:T(1024)(128)(4,1)S(1)} %pad.clone.2), kind=kOutput, calls=%fused_computation.52.clone.1 | convolution fusion | flops 1158675968 | bytes 20458500 | tf_op jit(solution)/shard_map/while/body/eval_jaxpr/rd,kd->rk/dot_general | solution.py:86
  178.8 8.5 %fusion.38 = f32[512]{0:T(512)S(1)} fusion(f32[512,8704]{1,0:T(8,128)} %get-tuple-element.167, f32[512]{0:T(512)S(1)} %get-tuple-element.168), kind=kLoop, calls=%fused_computation.6.clone.1 | loop fusion | flops 8912384 | bytes 17829888 | tf_op jit(solution)/shard_map/while/body/eval_jaxpr/reduce_sum | solution.py:99
  187.3 9.5 %fusion.39 = bf16[1,512,128]{2,1,0:T(8,128)(2,1)S(1)} fusion(bf16[8704,128]{1,0:T(8,128)(2,1)} %get-tuple-element.192, f32[512,8704]{1,0:T(8,128)} %get-tuple-element.167, f32[512]{0:T(512)S(1)} %fusion.38, f32[512]{0:T(512)S(1)} %get-tuple-element.168), kind=kOutput, calls=%fused_computation.9.clone.1 | convolution fusion | flops 1154285568 | bytes 20189184 | tf_op jit(solution)/shard_map/while/body/eval_jaxpr/dot_general | solution.py:100
  196.9 0.1 copy.81
  197.0 0.2 iota_compare_fusion.8
  197.2 0.1 broadcast_bitcast_fusion.2
  197.3 8.5 %fusion.37 = (f32[512]{0:T(512)S(1)}, f32[512,8704]{1,0:T(8,128)}) fusion(bf16[8704,128]{1,0:T(8,128)(2,1)S(1)} %get-tuple-element.191, bf16[4,512,128]{1,2,0:T(8,128)(2,1)S(1)} %get-tuple-element.190, s32[]{:T(128)} %get-tuple-element.178, pred[512,512]{1,0:T(32,128)(4,1)S(1)} %iota_compare_fusion.8, pred[8704]{0:T(1024)(128)(4,1)S(1)} %pad.clone.2), kind=kOutput, calls=%fused_computation.52.clone.1 | convolution fusion | flops 1158675968 | bytes 20458500 | tf_op jit(solution)/shard_map/while/body/eval_jaxpr/rd,kd->rk/dot_general | solution.py:86
  205.8 8.5 %fusion.38 = f32[512]{0:T(512)S(1)} fusion(f32[512,8704]{1,0:T(8,128)} %get-tuple-element.167, f32[512]{0:T(512)S(1)} %get-tuple-element.168), kind=kLoop, calls=%fused_computation.6.clone.1 | loop fusion | flops 8912384 | bytes 17829888 | tf_op jit(solution)/shard_map/while/body/eval_jaxpr/reduce_sum | solution.py:99
  214.3 9.5 %fusion.39 = bf16[1,512,128]{2,1,0:T(8,128)(2,1)S(1)} fusion(bf16[8704,128]{1,0:T(8,128)(2,1)} %get-tuple-element.192, f32[512,8704]{1,0:T(8,128)} %get-tuple-element.167, f32[512]{0:T(512)S(1)} %fusion.38, f32[512]{0:T(512)S(1)} %get-tuple-element.168), kind=kOutput, calls=%fused_computation.9.clone.1 | convolution fusion | flops 1154285568 | bytes 20189184 | tf_op jit(solution)/shard_map/while/body/eval_jaxpr/dot_general | solution.py:100
  223.9 0.1 copy.81
  224.0 7.2 %convolution_convert_fusion.2 = bf16[512,5120]{1,0:T(8,128)(2,1)} fusion(bf16[512,512]{0,1:T(8,128)(2,1)S(1)} %bitcast.61, bf16[512,5120]{1,0:T(8,128)(2,1)} %param.15), kind=kOutput, calls=%fused_computation.20 | convolution fusion | flops 2686976000 | bytes 11010048 | tf_op jit(solution)/shard_map/dot_general | solution.py:107
  231.9 0.1 fusion.20
  232.0 0.1 select_reduce_fusion.1
  232.1 0.7 copy.69
  232.8 7.7 %all-to-all-start.2 = ((s32[32,1,1]{2,1,0:T(1,128)}), s32[32,1,1]{2,1,0:T(1,128)S(1)}, u32[]{:S(2)}, u32[]{:S(2)}) async-start(s32[32,1,1]{2,1,0:T(1,128)} %copy.69), calls=%async_computation.3 | async-start | bytes 32768 | tf_op jit(solution)/shard_map/all_to_all | solution.py:68
  240.5 0.1 reshape.183
  240.6 2.2 convolution_convert_fusion.1
  242.8 4.7 %reshape.184 = bf16[32,1,128,2,128]{4,3,2,0,1:T(2,128)(2,1)} reshape(bf16[32,32768]{1,0:T(8,128)(2,1)} %convolution_convert_fusion.1) | data formatting | bytes 4194304 | tf_op jit(solution)/shard_map/reshape | solution.py:49
  247.5 8.4 %all-to-all-start.3 = ((bf16[32,1,128,2,128]{4,3,2,1,0:T(2,128)(2,1)}), bf16[32,1,128,2,128]{4,3,2,1,0:T(2,128)(2,1)}, u32[]{:S(2)}, u32[]{:S(2)}) async-start(bf16[32,1,128,2,128]{4,3,2,1,0:T(2,128)(2,1)} %bitcast.59), calls=%async_computation.4 | async-start | bytes 4194304 | tf_op jit(solution)/shard_map/all_to_all | solution.py:67
  255.8 2.8 reshape.186
  258.6 0.7 reduce.1
  259.3 0.1 fusion.15
  259.4 44.7 %all-to-all-done.3 = bf16[32,1,128,2,128]{4,3,2,1,0:T(2,128)(2,1)} async-done(((bf16[32,1,128,2,128]{4,3,2,1,0:T(2,128)(2,1)}), bf16[32,1,128,2,128]{4,3,2,1,0:T(2,128)(2,1)}, u32[]{:S(2)}, u32[]{:S(2)}) %all-to-all-start.3) | async-done | bytes 2097184 | tf_op jit(solution)/shard_map/all_to_all | solution.py:67
  304.1 4.5 %reshape.185 = bf16[32,32768]{1,0:T(8,128)(2,1)} reshape(bf16[32,1,128,2,128]{4,3,2,1,0:T(2,128)(2,1)} %all-to-all-done.3) | data formatting | bytes 4194304 | tf_op jit(solution)/shard_map/reshape | solution.py:118
  308.6 3.7 %fusion.11 = bf16[32,32768]{1,0:T(8,128)(2,1)} fusion(bf16[32,32768]{1,0:T(8,128)(2,1)S(1)} %copy-done.1, bf16[32,32768]{1,0:T(8,128)(2,1)} %reshape.185, pred[32]{0:T(512)(128)(4,1)S(1)} %fusion.15, s32[32]{0:T(128)S(1)} %reduce.1), kind=kOutput, calls=%fused_computation.19 | convolution fusion | flops 69207040 | bytes 6291616 | tf_op jit(solution)/shard_map/dot_general | solution.py:116
  312.3 4.4 %reshape.187 = bf16[32,128,2,128]{3,2,1,0:T(2,128)(2,1)} reshape(bf16[32,32768]{1,0:T(8,128)(2,1)} %fusion.11) | data formatting | bytes 4194304 | tf_op jit(solution)/shard_map/reshape | solution.py:123
  316.8 5.7 %reduce-scatter.2.cloned.1.call-done = bf16[64,5120]{1,0:T(8,128)(2,1)} async-done(((bf16[512,5120]{1,0:T(8,128)(2,1)}), bf16[64,5120]{1,0:T(8,128)(2,1)}) %reduce-scatter.2.cloned.1.call-update) | async-done | bytes 655376 | tf_op jit(solution)/shard_map/reduce_scatter | solution.py:106
  (38 shorter events, 0.3 us)
Async XLA Ops:
  42.5 7.3 %copy-start.4 = (bf16[512,512]{1,0:T(8,128)(2,1)S(1)}, bf16[512,512]{1,0:T(8,128)(2,1)}, u32[]{:S(2)}) copy-start(bf16[512,512]{1,0:T(8,128)(2,1)} %param.12) | copy-start | bytes 1572868
  42.5 7.5 %copy-start.2 = (bf16[512,2,128]{2,1,0:T(2,128)(2,1)S(1)}, bf16[512,2,128]{2,1,0:T(2,128)(2,1)}, u32[]{:S(2)}) copy-start(bf16[512,2,128]{2,1,0:T(2,128)(2,1)} %param.13) | copy-start | bytes 786436
  42.5 60.7 %all-to-all-start.1 = ((bf16[32,2,128,2,128]{4,2,1,3,0:T(8,128)(2,1)}), bf16[32,2,128,2,128]{4,2,1,3,0:T(8,128)(2,1)}, u32[]{:S(2)}, u32[]{:S(2)}) async-start(bf16[32,2,128,2,128]{4,2,1,3,0:T(8,128)(2,1)} %copy.62), calls=%async_computation.1 | async-start | bytes 8388608 | tf_op jit(solution)/shard_map/all_to_all | solution.py:55
  49.4 273.0 %reduce-scatter.2.cloned.1.call-start = ((), (), s32[]{:S(2)}) async-start(), calls=%async_computation.5 | async-start | bytes 5898240 | tf_op jit(solution)/shard_map/reduce_scatter | solution.py:106
  231.2 0.7 copy-start.5
  231.2 0.8 copy-start.6
  231.2 9.3 %copy-start.3 = (bf16[512,2,128]{2,1,0:T(2,128)(2,1)S(1)}, bf16[512,2,128]{2,1,0:T(2,128)(2,1)}, u32[]{:S(2)}) copy-start(bf16[512,2,128]{2,1,0:T(2,128)(2,1)} %param.13) | copy-start | bytes 786436
  232.8 14.7 %all-to-all-start.2 = ((s32[32,1,1]{2,1,0:T(1,128)}), s32[32,1,1]{2,1,0:T(1,128)S(1)}, u32[]{:S(2)}, u32[]{:S(2)}) async-start(s32[32,1,1]{2,1,0:T(1,128)} %copy.69), calls=%async_computation.3 | async-start | bytes 32768 | tf_op jit(solution)/shard_map/all_to_all | solution.py:68
  242.8 13.0 %copy-start = (bf16[32,128,2,128]{3,2,1,0:T(2,128)(2,1)S(1)}, bf16[32,128,2,128]{3,2,1,0:T(2,128)(2,1)}, u32[]{:S(2)}) copy-start(bf16[32,128,2,128]{3,2,1,0:T(2,128)(2,1)} %param.14) | copy-start | bytes 6291460
  247.5 56.7 %all-to-all-start.3 = ((bf16[32,1,128,2,128]{4,3,2,1,0:T(2,128)(2,1)}), bf16[32,1,128,2,128]{4,3,2,1,0:T(2,128)(2,1)}, u32[]{:S(2)}, u32[]{:S(2)}) async-start(bf16[32,1,128,2,128]{4,3,2,1,0:T(2,128)(2,1)} %bitcast.59), calls=%async_computation.4 | async-start | bytes 4194304 | tf_op jit(solution)/shard_map/all_to_all | solution.py:67
  258.6 50.0 %copy-start.1 = (bf16[32,32768]{1,0:T(8,128)(2,1)S(1)}, bf16[32,32768]{1,0:T(8,128)(2,1)}, u32[]{:S(2)}) copy-start(bf16[32,32768]{1,0:T(8,128)(2,1)} %reshape.186) | copy-start | bytes 6291460
Sparse Core Ops, SparseCore 0:
  231.3 91.0 reduce-scatter.1
where the time goes:
time: 331 us; the launch traced here: 329 us
  waiting for transfers between devices  103 us (31%)
  matrix products  84.9 us (26%)
  other arithmetic  47.9 us (14%)
  local copies, waits for them, and re-layouts  39.6 us (12%)
  starting transfers between devices  23.1 us (7%)
  between operations  15.6 us (5%)
  blocking collectives  15 us (5%)
    all_to_all x1, waiting for transfers between devices, on_device(): lax.all_to_all(saved_key_value[jnp.maximum(lax.all_to_all(requested, 'poo...  52.8 us
    all_to_all x1, waiting for transfers between devices, on_device(): lax.all_to_all(outgoing_blocks, 'pool', split_axis=0, concat_axis=0, tile...  44.7 us
    dot_general x4, matrix products, attend(): jnp.dot(normalized, value_rows, preferred_element_type=jnp.float32)  38 us
    reduce_sum x4, other arithmetic, attend(): jnp.sum(weights, axis=1, keepdims=True)  34.2 us
    dot_general x4, matrix products, attend(): jnp.einsum('rd,kd->rk', query_block, key_rows, preferred_element_type=jnp...  33.9 us
    gather x2, local copies, waits for them, and re-layouts, on_device(): saved_key_value[jnp.maximum(lax.all_to_all(requested, 'pool', split_axis=...  17.5 us
    all_to_all x1, blocking collectives, on_device(): lax.all_to_all(requested, 'pool', split_axis=0, concat_axis=0, tiled=True)  15 us
    all_to_all x1, starting transfers between devices, on_device(): lax.all_to_all(outgoing_blocks, 'pool', split_axis=0, concat_axis=0, tile...  8.36 us
  transfers between devices with their start and end apart: 4, of which 3 were waited for; matrix products, arithmetic and copies ran while one was open for 8% of the time, Pallas kernels for 0%

commit v1 on v0

v1 whole, which is shorter than its diff:
```python
import functools
import math

import jax
import jax.numpy as jnp
from jax import lax
from jax.experimental import pallas as pl
from jax.experimental.pallas import tpu as pltpu
from jax.sharding import PartitionSpec as P

HEAD = 128
CHUNK = 4
NT = (((1,), (1,)), ((), ()))
SMEM = pl.BlockSpec(memory_space=pltpu.SMEM)
VMEM = pl.BlockSpec(memory_space=pltpu.VMEM)
ANY = pl.BlockSpec(memory_space=pl.ANY)


def meta_kernel(dest_owner, dest_slot, evict, owner_ref, block_ref, meta_ref, order_ref):
    pool, entries = meta_ref.shape[0], owner_ref.shape[1]
    owner = jnp.broadcast_to(owner_ref[...], (pool, entries))
    block = jnp.broadcast_to(block_ref[...], (pool, entries))
    row = lax.broadcasted_iota(jnp.int32, (pool, entries), 0)
    col = lax.broadcasted_iota(jnp.int32, (pool, entries), 1)
    match = owner == row
    first = jnp.min(jnp.where(match, col, entries), axis=1, keepdims=True)
    want0 = jnp.sum(jnp.where(match & (col == first), block, 0), axis=1, keepdims=True)
    want1 = jnp.sum(jnp.where(match & (col > first), block, 0), axis=1, keepdims=True)
    place = 2 * row + jnp.where(col > first, 1, 0)
    order_ref[...] = jnp.sum(jnp.where(match, place, 0), axis=0, keepdims=True)
    lane = lax.broadcasted_iota(jnp.int32, (pool, 128), 1)
    out = jnp.where(lane == 0, want0, jnp.where(lane == 1, want1, 0))
    for b in range(4):
        out = jnp.where(lane == 2 + b, dest_owner[0, b], out)
        out = jnp.where(lane == 6 + b, dest_slot[0, b], out)
    out = jnp.where(lane == 10, evict[0], out)
    for o in range(pool):
        meta_ref[o] = out[o : o + 1]


def exchange_table(hist_owner, hist_block, dest_owner, dest_slot, evict, pool):
    return pl.pallas_call(
        meta_kernel,
        out_shape=(
            jax.ShapeDtypeStruct((pool, 1, 128), jnp.int32),
            jax.ShapeDtypeStruct(hist_owner.shape, jnp.int32),
        ),
        in_specs=[SMEM, SMEM, SMEM, VMEM, VMEM],
        out_specs=(VMEM, VMEM),
        name="table",
    )(dest_owner, dest_slot, evict, hist_owner, hist_block)


def gather_kernel(wanted, pool_ref, out_ref, sems):
    copies = []
    for i in range(out_ref.shape[0]):
        copies.append(
            pltpu.make_async_copy(
                pool_ref.at[wanted[i // 2, 0, i % 2]], out_ref.at[i], sems.at[i]
            )
        )
        copies[-1].start()
    for copy in copies:
        copy.wait()


def gather_blocks(wanted, pool_blocks):
    count = 2 * wanted.shape[0]
    return pl.pallas_call(
        gather_kernel,
        out_shape=jax.ShapeDtypeStruct((count,) + pool_blocks.shape[1:], pool_blocks.dtype),
        in_specs=[SMEM, ANY],
        out_specs=ANY,
        scratch_shapes=[pltpu.SemaphoreType.DMA((count,))],
        name="gather",
    )(wanted, pool_blocks)


def attend_kernel(order, length, base, q_ref, kv_ref, kn_ref, vn_ref, o_ref, sbuf, *, tok, split):
    c = math.log2(math.e) / math.sqrt(HEAD)
    heads = q_ref.shape[1] // HEAD
    per = heads // split
    rows = per * tok
    new = kn_ref.shape[0]
    qs = [
        jnp.concatenate(
            [q_ref[:, (s * per + h) * HEAD : (s * per + h + 1) * HEAD] for h in range(per)], axis=0
        )
        for s in range(split)
    ]

    def scores(k, q):
        return lax.dot_general(k, q, NT, preferred_element_type=jnp.float32)

    def update(state, s, vt):
        m, l, acc = state
        top = jnp.maximum(m, jnp.max(s, axis=0, keepdims=True))
        p = jnp.exp2(s * c - top * c)
        keep = jnp.exp2((m - top) * c)
        l = l * keep + jnp.sum(p, axis=0, keepdims=True)
        acc = acc * keep + jnp.dot(
            vt, p.astype(jnp.bfloat16), preferred_element_type=jnp.float32
        )
        return top, l, acc

    key = lax.broadcasted_iota(jnp.int32, (new, rows), 0)
    at = lax.broadcasted_iota(jnp.int32, (new, rows), 1) & (tok - 1)
    token = base[0] + at
    for b in range(1, tok // 128):
        token = jnp.where(at >= 128 * b, base[b] + at - 128 * b, token)
    state = []
    for s in range(split):
        sc = jnp.where(key <= token, scores(kn_ref[...], qs[s]), -jnp.inf)
        m = jnp.max(sc, axis=0, keepdims=True)
        p = jnp.exp2(sc * c - m * c)
        state.append(
            (
                m,
                jnp.sum(p, axis=0, keepdims=True),
                jnp.dot(vn_ref[...], p.astype(jnp.bfloat16), preferred_element_type=jnp.float32),
            )
        )

    def keys_of(i):
        return jnp.concatenate(
            [kv_ref[order[0, i * CHUNK + u], 0:128, :] for u in range(CHUNK)], axis=0
        )

    def values_of(i):
        return jnp.concatenate(
            [kv_ref[order[0, i * CHUNK + u], 128:256, :] for u in range(CHUNK)], axis=1
        )

    n = length[0]
    full = n // CHUNK
    last = kv_ref.shape[0] // CHUNK - 1
    for s in range(split):
        sbuf[0, s] = scores(keys_of(0), qs[s])

    def step(i, state, a):
        k = keys_of(jnp.minimum(i + 1, last))
        vt = values_of(i)
        out = []
        for s in range(split):
            sbuf[1 - a, s] = scores(k, qs[s])
            out.append(update(state[s], sbuf[a, s], vt))
        return tuple(out)

    state = lax.fori_loop(
        0, full // 2, lambda i, st: step(2 * i + 1, step(2 * i, st, 0), 1), tuple(state)
    )
    state = lax.fori_loop(full // 2 * 2, full, lambda i, st: step(i, st, 0), state)

    def tail(i, state):
        k, vt = keys_of(i), values_of(i)
        position = i * (CHUNK * 128) + lax.broadcasted_iota(jnp.int32, (CHUNK * 128, rows), 0)
        live = position < n * 128
        return tuple(
            update(state[s], jnp.where(live, scores(k, qs[s]), -jnp.inf), vt) for s in range(split)
        )

    state = lax.fori_loop(full, (n + CHUNK - 1) // CHUNK, tail, state)
    for s in range(split):
        m, l, acc = state[s]
        context = (acc / l).T.astype(jnp.bfloat16)
        for h in range(per):
            hh = s * per + h
            o_ref[:, hh * HEAD : (hh + 1) * HEAD] = context[h * tok : (h + 1) * tok]


def attend(q, kv, k_new, vt_new, order, length, base):
    tok, width = q.shape
    heads = width // HEAD
    split = 2 if tok > 128 else 1
    return pl.pallas_call(
        functools.partial(attend_kernel, tok=tok, split=split),
        out_shape=jax.ShapeDtypeStruct(q.shape, jnp.bfloat16),
        in_specs=[SMEM, SMEM, SMEM, VMEM, VMEM, VMEM, VMEM],
        out_specs=VMEM,
        scratch_shapes=[pltpu.VMEM((2, split, CHUNK * 128, heads // split * tok), jnp.float32)],
        compiler_params=pltpu.CompilerParams(vmem_limit_bytes=40 * 2**20),
        cost_estimate=pl.CostEstimate(
            flops=tok * heads * 8704 * 128 * 4, bytes_accessed=5 * 2**20, transcendentals=0
        ),
        name=f"attend{tok}",
    )(order, length, base, q, kv, k_new, vt_new)


def write_kernel(slots, saved_ref, fresh_ref, out_ref, sem, sems):
    whole = pltpu.make_async_copy(saved_ref, out_ref, sem)
    whole.start()
    whole.wait()
    for b in range(fresh_ref.shape[0]):

        @pl.when(slots[b] >= 0)
        def _(b=b):
            copy = pltpu.make_async_copy(fresh_ref.at[b], out_ref.at[slots[b]], sems.at[b])
            copy.start()
            copy.wait()


def write_back(slots, saved, fresh):
    return pl.pallas_call(
        write_kernel,
        out_shape=jax.ShapeDtypeStruct(saved.shape, saved.dtype),
        in_specs=[SMEM, ANY, ANY],
        out_specs=ANY,
        scratch_shapes=[pltpu.SemaphoreType.DMA, pltpu.SemaphoreType.DMA((fresh.shape[0],))],
        name="write",
    )(slots, saved, fresh)


def swap_pool(x):
    return lax.all_to_all(x, "pool", split_axis=0, concat_axis=0, tiled=True)


def on_device(
    queries,
    new_key_value,
    saved,
    out_weight,
    hist_owner,
    hist_block,
    hist_len,
    evict,
    dest_owner,
    dest_slot,
):
    pool = lax.axis_size("pool")
    me = lax.axis_index("pool")
    table, order = exchange_table(hist_owner, hist_block, dest_owner, dest_slot, evict, pool)
    told = swap_pool(table)
    pool_blocks = jnp.concatenate(
        [saved[:, :, 0, :], saved[:, :, 1, :].transpose(0, 2, 1)], axis=1
    )
    k_new = new_key_value[:, 0]
    vt_new = new_key_value[:, 1].T
    fetched = swap_pool(gather_blocks(told, pool_blocks).reshape(pool, 512, 128))
    kv = fetched.reshape(2 * pool, 256, 128)

    contexts = []
    for g in range(2):
        base = jnp.array([256 * g, 256 * g + 128], jnp.int32)
        contexts.append(
            attend(queries[256 * g : 256 * (g + 1)], kv, k_new, vt_new, order, hist_len, base)
        )
    contexts = jnp.concatenate(contexts, axis=0)
    attn_out = lax.psum_scatter(
        jnp.dot(contexts, out_weight, preferred_element_type=jnp.float32).astype(jnp.bfloat16),
        "tensor",
        scatter_dimension=0,
        tiled=True,
    )

    pieces = new_key_value.reshape(4, pool, -1).transpose(1, 0, 2)
    pieces, _ = lax.optimization_barrier((pieces, contexts))
    held = swap_pool(pieces)
    targets = told[:, 0, 2:6]
    chosen = targets.T[:, None, :] == jnp.arange(pool, dtype=jnp.int32)[None, :, None]
    onward = jnp.einsum(
        "bop,pbx->obx", chosen.astype(jnp.bfloat16), held, preferred_element_type=jnp.float32
    ).astype(jnp.bfloat16)
    fresh = swap_pool(onward).transpose(1, 0, 2).reshape((4,) + saved.shape[1:])
    mine = (targets == me) & (told[:, 0, 10:11] > 0)
    slots = jnp.max(jnp.where(mine, told[:, 0, 6:10], -1), axis=0)
    pool_out = write_back(slots, saved, fresh)
    return attn_out, pool_out


def solution(mesh):
    in_specs = (
        P("pool", "tensor"),
        P("pool", None, "tensor"),
        P("pool", None, None, "tensor"),
        P("tensor", None),
        P("pool", None),
        P("pool", None),
        P("pool"),
        P("pool"),
        P("pool", None),
        P("pool", None),
    )
    out_specs = (P(("pool", "tensor"), None), P("pool", None, None, "tensor"))
    return jax.shard_map(
        on_device, mesh=mesh, in_specs=in_specs, out_specs=out_specs, check_vma=False
    )
```

time: 331 us -> 380 us (1.15); the launches traced: 329 us -> 374 us
  Pallas kernels: 0 us -> 228 us
  matrix products: 84.9 us -> 4.95 us
  other arithmetic: 47.9 us -> 2.98 us
  waiting for transfers between devices: 103 us -> 71.1 us
  local copies, waits for them, and re-layouts: 39.6 us -> 16.6 us
  blocking collectives: 15 us -> 0 us
  starting transfers between devices: 23.1 us -> 34.7 us
    pallas_call x0 -> x5, Pallas kernels: none -> 228 us  [the longest x1 130 us: gather_blocks(): pl.pallas_call(gather_kernel, out_shape=jax.ShapeDtypeStruct((count,) + p...]
    dot_general x10 -> x1, matrix products: 77.7 us -> 0.22 us  [on_device(): jnp.einsum('bop,pbx->obx', chosen.astype(jnp.bfloat16), held, preferred_e...]
    reduce_sum x6 -> x0, other arithmetic: 35 us -> none  [the longest x4 34.2 us: attend(): jnp.sum(weights, axis=1, keepdims=True)]
    all_to_all x3 -> x4, waiting for transfers between devices: 97.5 us -> 71.1 us  [swap_pool(): return lax.all_to_all(x, 'pool', split_axis=0, concat_axis=0, tiled=True)]
    gather x2 -> x0, local copies, waits for them, and re-layouts: 17.5 us -> none  [on_device(): saved_key_value[jnp.maximum(lax.all_to_all(requested, 'pool', split_axis=...]
    reshape x5 -> x2, local copies, waits for them, and re-layouts: 16.5 us -> 1.07 us  [the longest x1 0.89 us: on_device(): fresh = swap_pool(onward).transpose(1, 0, 2).reshape((4,) + saved.shape[1:])]
    all_to_all x1 -> x0, blocking collectives: 15 us -> none  [on_device(): lax.all_to_all(requested, 'pool', split_axis=0, concat_axis=0, tiled=True)]
    all_to_all x3 -> x4, starting transfers between devices: 23 us -> 34.7 us  [swap_pool(): return lax.all_to_all(x, 'pool', split_axis=0, concat_axis=0, tiled=True)]
  transfers between devices with their start and end apart: 4 -> 5, of which waited for: 3 -> 3; matrix products, arithmetic and copies ran while one was open for 8% -> 5% of each run, Pallas kernels for 0% -> 19%
where the time goes in v1:
time: 380 us; the launch traced here: 374 us
  Pallas kernels  228 us (60%)
  waiting for transfers between devices  71.1 us (19%)
  starting transfers between devices  34.7 us (9%)
  local copies, waits for them, and re-layouts  16.6 us (4%)
  between operations  15.6 us (4%)
  matrix products  4.95 us (1%)
    pallas_call x1, Pallas kernels, gather_blocks(): pl.pallas_call(gather_kernel, out_shape=jax.ShapeDtypeStruct((count,) + p...  130 us
    pallas_call x1, Pallas kernels, write_back(): pl.pallas_call(write_kernel, out_shape=jax.ShapeDtypeStruct(saved.shape,...  71.5 us
    all_to_all x4, waiting for transfers between devices, swap_pool(): return lax.all_to_all(x, 'pool', split_axis=0, concat_axis=0, tiled=True)  71.1 us
    all_to_all x4, starting transfers between devices, swap_pool(): return lax.all_to_all(x, 'pool', split_axis=0, concat_axis=0, tiled=True)  34.7 us
    pallas_call x2, Pallas kernels, attend(): pl.pallas_call(functools.partial(attend_kernel, tok=tok, split=split), ou...  25.5 us
  transfers between devices with their start and end apart: 5, of which 3 were waited for; matrix products, arithmetic and copies ran while one was open for 5% of the time, Pallas kernels for 19%

profile of v1, /device:TPU:4, one launch (start us, length us, event | category | flops | bytes accessed | tf_op | source)
XLA Modules:
  0.0 374.2 jit_solution(5502941817689249941)
XLA Ops:
  7.8 1.6 table.1
  9.4 9.0 %all-to-all-start = ((s32[32,1,128]{2,1,0:T(1,128)}), s32[32,1,128]{2,1,0:T(1,128)S(1)}, u32[]{:S(2)}, u32[]{:S(2)}) async-start(s32[32,1,128]{2,1,0:T(1,128)} %get-tuple-element.6), calls=%async_computation | async-start | bytes 32768 | tf_op jit(solution)/shard_map/all_to_all | solution.py:214
  18.3 7.0 %fusion.5 = (bf16[32,128,1,128]{3,2,1,0:T(2,128)(2,1)S(1)}, bf16[32,128,1,128]{3,2,1,0:T(2,128)(2,1)}) fusion(bf16[32,128,2,128]{3,2,1,0:T(2,128)(2,1)} %saved_ref.1), kind=kLoop, calls=%fused_computation.16 | loop fusion | bytes 4194304 | tf_op jit(solution)/shard_map/slice | solution.py:234
  25.3 5.0 %copy.46 = bf16[32,128,1,128]{1,3,0,2:T(8,128)(2,1)S(1)} copy(bf16[32,128,1,128]{3,2,1,0:T(2,128)(2,1)} %get-tuple-element.9) | data formatting | bytes 2097152
  30.3 0.2 copy.53
  30.5 1.5 pad_maximum_fusion.pool_ref
  32.0 0.0 all-to-all-done.wanted
  32.0 0.0 copy-start.4
  32.0 0.6 copy-done.4
  32.6 129.7 %gather.1 = bf16[64,256,128]{2,1,0:T(8,128)(2,1)} custom-call(s32[32,1,128]{2,1,0:T(1,128)} %copy-done.4, bf16[32,256,128]{2,1,0:T(8,128)(2,1)} %pad_maximum_fusion.pool_ref), custom_call_target="tpu_custom_call" | custom-call | tf_op jit(solution)/shard_map/gather/pallas_call | solution.py:69
  162.3 0.0 copy-start.2
  162.3 0.0 copy-start.3
  162.3 0.0 copy-start
  162.3 8.5 %all-to-all-start.1 = ((bf16[32,512,128]{2,1,0:T(8,128)(2,1)}), bf16[32,512,128]{2,1,0:T(8,128)(2,1)}, u32[]{:S(2)}, u32[]{:S(2)}) async-start(bf16[32,512,128]{2,1,0:T(8,128)(2,1)} %bitcast.35), calls=%async_computation.1 | async-start | bytes 8388608 | tf_op jit(solution)/shard_map/all_to_all | solution.py:214
  170.8 0.0 reduce-scatter.2.cloned.1.call-start
  170.9 0.0 copy-done.2
  170.9 0.4 fusion.7
  171.3 0.1 copy.48
  172.1 0.0 copy-done.3
  172.1 53.8 %all-to-all-done.1 = bf16[32,512,128]{2,1,0:T(8,128)(2,1)} async-done(((bf16[32,512,128]{2,1,0:T(8,128)(2,1)}), bf16[32,512,128]{2,1,0:T(8,128)(2,1)}, u32[]{:S(2)}, u32[]{:S(2)}) %all-to-all-start.1) | async-done | bytes 4194336 | tf_op jit(solution)/shard_map/all_to_all | solution.py:214
  226.0 0.0 copy-done
  226.0 0.0 copy-start.1
  226.0 0.0 slice-start
  226.0 12.7 %attend256.2 = bf16[256,512]{1,0:T(8,128)(2,1)S(1)} custom-call(s32[1,64]{1,0:T(1,128)S(1)} %copy-done, s32[1]{0:T(128)S(6)} %copy.55.length, s32[2]{0:T(128)S(1)} %iota_multiply_fusion.base, bf16[256,512]{1,0:T(8,128)(2,1)S(1)} %get-tuple-element.10.q_ref, bf16[64,256,128]{2,1,0:T(8,128)(2,1)} %bitcast.4.kv_ref, bf16[512,128]{1,0:T(8,128)(2,1)S(1)} %bitcast.31, ...), custom_call_target="tpu_custom_call" | custom-call | flops 4563402752 | bytes 5242880 | tf_op jit(solution)/shard_map/attend256/pallas_call | solution.py:175
  238.7 0.0 slice-start.1
  238.7 0.0 copy-done.1
  238.7 12.8 %attend256.3 = bf16[256,512]{1,0:T(8,128)(2,1)S(1)} custom-call(s32[1,64]{1,0:T(1,128)S(1)} %copy-done, s32[1]{0:T(128)S(6)} %copy.55.length, s32[2]{0:T(128)S(1)} %copy-done.1, bf16[256,512]{1,0:T(8,128)(2,1)S(1)} %get-tuple-element.11.q_ref, bf16[64,256,128]{2,1,0:T(8,128)(2,1)} %bitcast.4.kv_ref, bf16[512,128]{1,0:T(8,128)(2,1)S(1)} %bitcast.32, ...), custom_call_target="tpu_custom_call" | custom-call | flops 4563402752 | bytes 5242880 | tf_op jit(solution)/shard_map/attend256/pallas_call | solution.py:175
  251.5 0.0 slice-done
  251.5 0.0 slice-done.1
  251.5 4.7 %convolution_convert_fusion = bf16[512,5120]{1,0:T(8,128)(2,1)} fusion(bf16[512,5120]{1,0:T(8,128)(2,1)S(1)} %bitcast.42, bf16[256,512]{1,0:T(8,128)(2,1)S(1)} %attend256.3, bf16[256,512]{1,0:T(8,128)(2,1)S(1)} %attend256.2), kind=kOutput, calls=%fused_computation | convolution fusion | flops 2688024576 | bytes 11010048 | tf_op jit(solution)/shard_map/dot_general | solution.py:249
  256.3 0.0 copy-start.5
  256.3 0.0 reduce-scatter.2.cloned.1.call-update
  256.3 0.2 reshape.28
  256.5 0.9 copy.41
  257.4 11.5 %all-to-all-start.2 = ((bf16[32,4,1024]{2,1,0:T(4,128)(2,1)}), bf16[32,4,1024]{2,1,0:T(4,128)(2,1)S(1)}, u32[]{:S(2)}, u32[]{:S(2)}) async-start(bf16[32,4,1024]{2,1,0:T(4,128)(2,1)} %copy.41), calls=%async_computation.3 | async-start | bytes 524288 | tf_op jit(solution)/shard_map/all_to_all | solution.py:214
  268.9 0.0 copy-done.5
  268.9 0.1 fusion.8
  269.0 0.1 copy.39
  269.1 7.0 %all-to-all-done.2 = bf16[32,4,1024]{2,1,0:T(4,128)(2,1)S(1)} async-done(((bf16[32,4,1024]{2,1,0:T(4,128)(2,1)}), bf16[32,4,1024]{2,1,0:T(4,128)(2,1)S(1)}, u32[]{:S(2)}, u32[]{:S(2)}) %all-to-all-start.2) | async-done | bytes 262176 | tf_op jit(solution)/shard_map/all_to_all | solution.py:214
  276.1 0.2 fusion
  276.3 0.9 copy.43
  277.3 5.8 %all-to-all-start.3 = ((bf16[32,4,1024]{2,1,0:T(4,128)(2,1)}), bf16[32,4,1024]{2,1,0:T(4,128)(2,1)S(1)}, u32[]{:S(2)}, u32[]{:S(2)}) async-start(bf16[32,4,1024]{2,1,0:T(4,128)(2,1)} %copy.43), calls=%async_computation.4 | async-start | bytes 524288 | tf_op jit(solution)/shard_map/all_to_all | solution.py:214
  283.0 0.1 copy.40
  283.1 0.7 compare_reduce_fusion
  283.8 0.7 fusion.3.slots
  284.5 10.3 %all-to-all-done.3 = bf16[32,4,1024]{2,1,0:T(4,128)(2,1)S(1)} async-done(((bf16[32,4,1024]{2,1,0:T(4,128)(2,1)}), bf16[32,4,1024]{2,1,0:T(4,128)(2,1)S(1)}, u32[]{:S(2)}, u32[]{:S(2)}) %all-to-all-start.3) | async-done | bytes 262176 | tf_op jit(solution)/shard_map/all_to_all | solution.py:214
  294.8 0.1 copy.44
  294.9 0.9 reshape.29.fresh_ref
  295.8 71.5 %write.1 = bf16[32,128,2,128]{3,2,1,0:T(2,128)(2,1)} custom-call(s32[4]{0:T(128)} %fusion.3.slots, bf16[32,128,2,128]{3,2,1,0:T(2,128)(2,1)} %saved_ref.1, bf16[4,128,2,128]{3,2,1,0:T(2,128)(2,1)} %reshape.29.fresh_ref), custom_call_target="tpu_custom_call" | custom-call | tf_op jit(solution)/shard_map/write/pallas_call | solution.py:203
  367.3 0.0 reduce-scatter.2.cloned.1.call-done
  (4 shorter events, 0.1 us)
Async XLA Ops:
  9.4 22.7 %all-to-all-start = ((s32[32,1,128]{2,1,0:T(1,128)}), s32[32,1,128]{2,1,0:T(1,128)S(1)}, u32[]{:S(2)}, u32[]{:S(2)}) async-start(s32[32,1,128]{2,1,0:T(1,128)} %get-tuple-element.6), calls=%async_computation | async-start | bytes 32768 | tf_op jit(solution)/shard_map/all_to_all | solution.py:214
  32.0 0.6 copy-start.4
  162.3 8.6 %copy-start.2 = (bf16[512,2,128]{2,1,0:T(2,128)(2,1)S(1)}, bf16[512,2,128]{2,1,0:T(2,128)(2,1)}, u32[]{:S(2)}) copy-start(bf16[512,2,128]{2,1,0:T(2,128)(2,1)} %param.13) | copy-start | bytes 786436
  162.3 9.8 %copy-start.3 = (bf16[512,512]{1,0:T(8,128)(2,1)S(1)}, bf16[512,512]{1,0:T(8,128)(2,1)}, u32[]{:S(2)}) copy-start(bf16[512,512]{1,0:T(8,128)(2,1)} %param.12) | copy-start | bytes 1572868
  162.3 63.6 %copy-start = (s32[1,64]{1,0:T(1,128)S(1)}, s32[1,64]{1,0:T(1,128)}, u32[]{:S(2)}) copy-start(s32[1,64]{1,0:T(1,128)} %get-tuple-element.5.order) | copy-start | bytes 772
  162.3 63.6 %all-to-all-start.1 = ((bf16[32,512,128]{2,1,0:T(8,128)(2,1)}), bf16[32,512,128]{2,1,0:T(8,128)(2,1)}, u32[]{:S(2)}, u32[]{:S(2)}) async-start(bf16[32,512,128]{2,1,0:T(8,128)(2,1)} %bitcast.35), calls=%async_computation.1 | async-start | bytes 8388608 | tf_op jit(solution)/shard_map/all_to_all | solution.py:214
  170.8 196.5 %reduce-scatter.2.cloned.1.call-start = ((), (), s32[]{:S(2)}) async-start(), calls=%async_computation.5 | async-start | bytes 5898240 | tf_op jit(solution)/shard_map/reduce_scatter | solution.py:248
  226.0 12.7 %copy-start.1 = (s32[2]{0:T(128)S(1)}, s32[2]{0:T(128)}, u32[]{:S(2)}) copy-start(s32[2]{0:T(128)} %constant.18.clone.base) | copy-start | bytes 28
  226.0 25.5 %slice-start = ((s8[5242880]{0:T(1024)(128)(4,1)}), s8[4194304]{0:T(1024)(128)(4,1)S(1)}, s32[]{:S(2)}) async-start(s8[5242880]{0:T(1024)(128)(4,1)} %bitcast.41), calls=%async_computation.6 | async-start | bytes 8388608
  238.7 12.8 %slice-start.1 = ((s8[5242880]{0:T(1024)(128)(4,1)}), s8[1048576]{0:T(1024)(128)(4,1)S(1)}, s32[]{:S(2)}) async-start(s8[5242880]{0:T(1024)(128)(4,1)} %bitcast.41), calls=%async_computation.7 | async-start | bytes 2097152
  256.3 12.6 %copy-start.5 = (s32[32,1,128]{2,1,0:T(1,128)S(1)}, s32[32,1,128]{2,1,0:T(1,128)}, u32[]{:S(2)}) copy-start(s32[32,1,128]{2,1,0:T(1,128)} %copy-done.4) | copy-start | bytes 49156
  257.4 18.7 %all-to-all-start.2 = ((bf16[32,4,1024]{2,1,0:T(4,128)(2,1)}), bf16[32,4,1024]{2,1,0:T(4,128)(2,1)S(1)}, u32[]{:S(2)}, u32[]{:S(2)}) async-start(bf16[32,4,1024]{2,1,0:T(4,128)(2,1)} %copy.41), calls=%async_computation.3 | async-start | bytes 524288 | tf_op jit(solution)/shard_map/all_to_all | solution.py:214
  277.3 17.5 %all-to-all-start.3 = ((bf16[32,4,1024]{2,1,0:T(4,128)(2,1)}), bf16[32,4,1024]{2,1,0:T(4,128)(2,1)S(1)}, u32[]{:S(2)}, u32[]{:S(2)}) async-start(bf16[32,4,1024]{2,1,0:T(4,128)(2,1)} %copy.43), calls=%async_computation.4 | async-start | bytes 524288 | tf_op jit(solution)/shard_map/all_to_all | solution.py:214
Sparse Core Ops, SparseCore 0:
  256.4 74.1 reduce-scatter.1

commit v2 on v1

v2 whole, which is shorter than its diff:
```python
import functools
import math

import jax
import jax.numpy as jnp
from jax import lax
from jax.experimental import pallas as pl
from jax.experimental.pallas import tpu as pltpu
from jax.sharding import PartitionSpec as P

HEAD = 128
CHUNK = 4
NT = (((1,), (1,)), ((), ()))
SMEM = pl.BlockSpec(memory_space=pltpu.SMEM)
VMEM = pl.BlockSpec(memory_space=pltpu.VMEM)
ANY = pl.BlockSpec(memory_space=pl.ANY)


def meta_kernel(dest_owner, dest_slot, evict, owner_ref, block_ref, meta_ref, order_ref):
    pool, entries = meta_ref.shape[0], owner_ref.shape[1]
    owner = jnp.broadcast_to(owner_ref[...], (pool, entries))
    block = jnp.broadcast_to(block_ref[...], (pool, entries))
    row = lax.broadcasted_iota(jnp.int32, (pool, entries), 0)
    col = lax.broadcasted_iota(jnp.int32, (pool, entries), 1)
    match = owner == row
    first = jnp.min(jnp.where(match, col, entries), axis=1, keepdims=True)
    want0 = jnp.sum(jnp.where(match & (col == first), block, 0), axis=1, keepdims=True)
    want1 = jnp.sum(jnp.where(match & (col > first), block, 0), axis=1, keepdims=True)
    place = 2 * row + jnp.where(col > first, 1, 0)
    order_ref[...] = jnp.sum(jnp.where(match, place, 0), axis=0, keepdims=True)
    lane = lax.broadcasted_iota(jnp.int32, (pool, 128), 1)
    out = jnp.where(lane == 0, want0, jnp.where(lane == 1, want1, 0))
    for b in range(4):
        out = jnp.where(lane == 2 + b, dest_owner[0, b], out)
        out = jnp.where(lane == 6 + b, dest_slot[0, b], out)
    out = jnp.where(lane == 10, evict[0], out)
    for o in range(pool):
        meta_ref[o] = out[o : o + 1]


def exchange_table(hist_owner, hist_block, dest_owner, dest_slot, evict, pool):
    return pl.pallas_call(
        meta_kernel,
        out_shape=(
            jax.ShapeDtypeStruct((pool, 1, 128), jnp.int32),
            jax.ShapeDtypeStruct(hist_owner.shape, jnp.int32),
        ),
        in_specs=[SMEM, SMEM, SMEM, VMEM, VMEM],
        out_specs=(VMEM, VMEM),
        name="table",
    )(dest_owner, dest_slot, evict, hist_owner, hist_block)


def split_kernel(x_ref, o_ref):
    row = lax.broadcasted_iota(jnp.int32, (128, 256), 0)
    source = lax.broadcasted_iota(jnp.int32, (128, 256), 1)
    pick_k = jnp.where(source == 2 * row, 1.0, 0.0).astype(jnp.bfloat16)
    pick_v = jnp.where(source == 2 * row + 1, 1.0, 0.0).astype(jnp.bfloat16)
    for b in range(x_ref.shape[0]):
        x = x_ref[b]
        k = jnp.dot(pick_k, x, preferred_element_type=jnp.float32)
        v = jnp.dot(pick_v, x, preferred_element_type=jnp.float32)
        o_ref[b, 0:128, :] = k.astype(jnp.bfloat16)
        o_ref[b, 128:256, :] = v.T.astype(jnp.bfloat16)


def split_blocks(x):
    return pl.pallas_call(
        split_kernel,
        out_shape=jax.ShapeDtypeStruct(x.shape, x.dtype),
        in_specs=[VMEM],
        out_specs=VMEM,
        compiler_params=pltpu.CompilerParams(vmem_limit_bytes=12 * 2**20),
        name=f"split{x.shape[0]}",
    )(x)


def gather_kernel(wanted, pool_ref, pieces_ref, out_ref, sems):
    copies = []
    pool = out_ref.shape[0]
    for p in range(pool):
        for r in range(2):
            copies.append(
                pltpu.make_async_copy(
                    pool_ref.at[wanted[p, 0, r]],
                    out_ref.at[p, pl.ds(256 * r, 256)],
                    sems.at[2 * p + r],
                )
            )
            copies[-1].start()
    copies.append(
        pltpu.make_async_copy(
            pieces_ref, out_ref.at[:, pl.ds(512, pieces_ref.shape[1])], sems.at[2 * pool]
        )
    )
    copies[-1].start()
    for copy in copies:
        copy.wait()


def gather_blocks(wanted, pool_blocks, pieces):
    pool = wanted.shape[0]
    return pl.pallas_call(
        gather_kernel,
        out_shape=jax.ShapeDtypeStruct((pool, 512 + pieces.shape[1], 128), pool_blocks.dtype),
        in_specs=[SMEM, VMEM, VMEM],
        out_specs=ANY,
        scratch_shapes=[pltpu.SemaphoreType.DMA((2 * pool + 1,))],
        name="gather",
    )(wanted, pool_blocks, pieces)


def attend_kernel(
    order, length, base, q_ref, kv_ref, new_ref, mine_ref, theirs_ref, sbuf, *, group, tok
):
    c = math.log2(math.e) / math.sqrt(HEAD)
    heads = q_ref.shape[1] // HEAD
    rows = heads * tok
    new_blocks = new_ref.shape[0]
    new = new_blocks * 128
    parts = base.shape[1]
    part = tok // parts
    q = jnp.concatenate(
        [
            q_ref[pl.ds(pl.multiple_of(base[group, i], part), part), h * HEAD : (h + 1) * HEAD]
            for h in range(heads)
            for i in range(parts)
        ],
        axis=0,
    )

    def scores(k):
        return lax.dot_general(k, q, NT, preferred_element_type=jnp.float32)

    def update(state, s, vt):
        m, l, acc = state
        top = jnp.maximum(m, jnp.max(s, axis=0, keepdims=True))
        p = jnp.exp2(s * c - top * c)
        keep = jnp.exp2((m - top) * c)
        l = l * keep + jnp.sum(p, axis=0, keepdims=True)
        acc = acc * keep + jnp.dot(
            vt, p.astype(jnp.bfloat16), preferred_element_type=jnp.float32
        )
        return top, l, acc

    key = lax.broadcasted_iota(jnp.int32, (new, rows), 0)
    at = lax.broadcasted_iota(jnp.int32, (1, rows), 1) & (tok - 1)
    token = base[group, 0] + at
    for i in range(1, parts):
        token = jnp.where(at >= part * i, base[group, i] + at - part * i, token)
    k_new = jnp.concatenate([new_ref[i, 0:128, :] for i in range(new_blocks)], axis=0)
    vt_new = jnp.concatenate([new_ref[i, 128:256, :] for i in range(new_blocks)], axis=1)
    s = jnp.where(key <= token, scores(k_new), -jnp.inf)
    m = jnp.max(s, axis=0, keepdims=True)
    p = jnp.exp2(s * c - m * c)
    state = (
        m,
        jnp.sum(p, axis=0, keepdims=True),
        jnp.dot(vt_new, p.astype(jnp.bfloat16), preferred_element_type=jnp.float32),
    )

    def half(i, u, value):
        place = order[0, i * CHUNK + u]
        start = pl.multiple_of((place % 2) * 256 + 128 * value, 128)
        return kv_ref[place // 2, pl.ds(start, 128), :]

    def keys_of(i):
        return jnp.concatenate([half(i, u, 0) for u in range(CHUNK)], axis=0)

    def values_of(i):
        return jnp.concatenate([half(i, u, 1) for u in range(CHUNK)], axis=1)

    n = length[0]
    full = n // CHUNK
    last = order.shape[1] // CHUNK - 1
    sbuf[0] = scores(keys_of(0))

    def step(i, state, a):
        sbuf[1 - a] = scores(keys_of(jnp.minimum(i + 1, last)))
        return update(state, sbuf[a], values_of(i))

    state = lax.fori_loop(
        0, full // 2, lambda i, st: step(2 * i + 1, step(2 * i, st, 0), 1), state
    )
    state = lax.fori_loop(full // 2 * 2, full, lambda i, st: step(i, st, 0), state)

    def tail(i, state):
        position = i * (CHUNK * 128) + lax.broadcasted_iota(jnp.int32, (CHUNK * 128, rows), 0)
        s = jnp.where(position < n * 128, scores(keys_of(i)), -jnp.inf)
        return update(state, s, values_of(i))

    m, l, acc = lax.fori_loop(full, (n + CHUNK - 1) // CHUNK, tail, state)
    context = (acc / l).T.astype(jnp.bfloat16)
    own = tok // 2
    for h in range(heads):
        mine_ref[:, h * HEAD : (h + 1) * HEAD] = context[h * tok : h * tok + own]
        theirs_ref[:, h * HEAD : (h + 1) * HEAD] = context[h * tok + own : (h + 1) * tok]


def attend(queries, kv, fresh, order, length, base, group):
    width = queries.shape[1]
    tok = queries.shape[0] // base.shape[0]
    heads = width // HEAD
    out = jax.ShapeDtypeStruct((tok // 2, width), jnp.bfloat16)
    return pl.pallas_call(
        functools.partial(attend_kernel, group=group, tok=tok),
        out_shape=(out, out),
        in_specs=[SMEM, SMEM, SMEM, VMEM, VMEM, VMEM],
        out_specs=(VMEM, VMEM),
        scratch_shapes=[pltpu.VMEM((2, CHUNK * 128, heads * tok), jnp.float32)],
        compiler_params=pltpu.CompilerParams(vmem_limit_bytes=16 * 2**20),
        cost_estimate=pl.CostEstimate(
            flops=tok * heads * 8704 * 128 * 4, bytes_accessed=5 * 2**20, transcendentals=0
        ),
        name=f"attend{group}",
    )(order, length, base, queries, kv, fresh)


def project_kernel(a_ref, b_ref, wa_ref, wb_ref, *refs):
    arrived, (up_ref, down_ref) = refs[:-2], refs[-2:]
    half = a_ref.shape[0] // 2
    tile = 512
    for j in range(wa_ref.shape[1] // tile):
        cols = slice(j * tile, (j + 1) * tile)
        total = jnp.dot(a_ref[...], wa_ref[:, cols], preferred_element_type=jnp.float32)
        total += jnp.dot(b_ref[...], wb_ref[:, cols], preferred_element_type=jnp.float32)
        up, down = total[:half], total[half:]
        if arrived:
            up += arrived[0][:, cols].astype(jnp.float32)
            down += arrived[1][:, cols].astype(jnp.float32)
        up_ref[:, cols] = up.astype(jnp.bfloat16)
        down_ref[:, cols] = down.astype(jnp.bfloat16)


def project(a, b, wa, wb, *arrived):
    out = jax.ShapeDtypeStruct((a.shape[0] // 2, wa.shape[1]), jnp.bfloat16)
    return pl.pallas_call(
        project_kernel,
        out_shape=(out, out),
        in_specs=[VMEM] * (4 + len(arrived)),
        out_specs=(VMEM, VMEM),
        cost_estimate=pl.CostEstimate(
            flops=4 * a.size * wa.shape[1], bytes_accessed=11 * 2**20, transcendentals=0
        ),
        name=f"project{len(arrived)}",
    )(a, b, wa, wb, *arrived)


def copy_kernel(x_ref, o_ref, buf, sem):
    for source, target in ((x_ref, buf), (buf, o_ref)):
        copy = pltpu.make_async_copy(source, target, sem)
        copy.start()
        copy.wait()


def copy_pool(x):
    return pl.pallas_call(
        copy_kernel,
        out_shape=jax.ShapeDtypeStruct(x.shape, x.dtype),
        in_specs=[ANY],
        out_specs=ANY,
        scratch_shapes=[pltpu.VMEM(x.shape, x.dtype), pltpu.SemaphoreType.DMA],
        name="copy_pool",
    )(x)


def write_kernel(slots, fresh_ref, kept_ref, out_ref, sems):
    del kept_ref
    for b in range(fresh_ref.shape[0]):

        @pl.when(slots[b] >= 0)
        def _(b=b):
            copy = pltpu.make_async_copy(fresh_ref.at[b], out_ref.at[slots[b]], sems.at[b])
            copy.start()
            copy.wait()


def write_back(slots, fresh, kept):
    return pl.pallas_call(
        write_kernel,
        out_shape=jax.ShapeDtypeStruct(kept.shape, kept.dtype),
        in_specs=[SMEM, VMEM, ANY],
        out_specs=ANY,
        input_output_aliases={2: 0},
        scratch_shapes=[pltpu.SemaphoreType.DMA((fresh.shape[0],))],
        name="write",
    )(slots, fresh, kept)


def swap_pool(x):
    return lax.all_to_all(x, "pool", split_axis=0, concat_axis=0, tiled=True)


def on_device(
    queries,
    new_key_value,
    saved,
    out_weight,
    hist_owner,
    hist_block,
    hist_len,
    evict,
    dest_owner,
    dest_slot,
):
    pool = lax.axis_size("pool")
    me = lax.axis_index("pool")
    chips = lax.axis_size("tensor") // 2
    chip, core = lax.axis_index("tensor") // 2, lax.axis_index("tensor") % 2
    other_core = [(2 * z + c, 2 * z + 1 - c) for z in range(chips) for c in range(2)]
    upward = [(2 * z + c, 2 * ((z + 1) % chips) + c) for z in range(chips) for c in range(2)]
    downward = [(target, source) for source, target in upward]
    swap = functools.partial(lax.ppermute, axis_name="tensor", perm=other_core)
    send_up = functools.partial(lax.ppermute, axis_name="tensor", perm=upward)
    send_down = functools.partial(lax.ppermute, axis_name="tensor", perm=downward)

    def part(offset, c, half):
        return 128 * ((chip + offset) % chips) + 64 * c + 32 * half

    plan = (((2, 0), (2, 1)), ((1, 1), (3, 0)), ((1, 0), (3, 1)), ((0, 0), (0, 1)))
    base = jnp.stack(
        [
            jnp.stack([part(o, c, h) for c in (core, 1 - core) for o, h in parts])
            for parts in plan
        ]
    ).astype(jnp.int32)

    table, order = exchange_table(hist_owner, hist_block, dest_owner, dest_slot, evict, pool)
    told = swap_pool(table)
    pool_blocks = split_blocks(saved.reshape(-1, 256, 128))
    fresh = split_blocks(new_key_value.reshape(-1, 256, 128))
    pieces = new_key_value.reshape(4, pool, 8, 128).transpose(1, 0, 2, 3).reshape(pool, 32, 128)
    kv = swap_pool(gather_blocks(told, pool_blocks, pieces))
    other_weight = swap(out_weight)
    kept = copy_pool(saved.reshape(-1, 256, 128))

    def contexts(group, after):
        first, _ = lax.optimization_barrier((order, after))
        mine, theirs = attend(queries, kv, fresh, first, hist_len, base, group)
        return mine, swap(theirs)

    up, down = project(*contexts(0, order), out_weight, other_weight)
    through_up, through_down = send_up(up), send_down(down)
    up, down = project(*contexts(1, up), out_weight, other_weight)
    near_up, near_down = send_up(up), send_down(down)
    up, down = project(*contexts(2, up), out_weight, other_weight, through_up, through_down)
    far_up, far_down = send_up(up), send_down(down)

    held, _ = lax.optimization_barrier((kv[:, 512:], up))
    held = held.reshape(pool, 4, -1)
    targets = told[:, 0, 2:6]
    chosen = targets.T[:, None, :] == jnp.arange(pool, dtype=jnp.int32)[None, :, None]
    onward = jnp.einsum(
        "bop,pbx->obx", chosen.astype(jnp.bfloat16), held, preferred_element_type=jnp.float32
    ).astype(jnp.bfloat16)
    returned = swap_pool(onward).reshape(pool, 4, 8, 128).transpose(1, 0, 2, 3)
    mine = (targets == me) & (told[:, 0, 10:11] > 0)
    slots = jnp.max(jnp.where(mine, told[:, 0, 6:10], -1), axis=0)

    top, bottom = project(*contexts(3, up), out_weight, other_weight)
    pool_out = write_back(slots, returned.reshape(4, 256, 128), kept).reshape(saved.shape)
    wide = lambda x: x.astype(jnp.float32)
    attn_out = jnp.concatenate(
        [
            wide(top) + wide(far_up) + wide(near_down),
            wide(bottom) + wide(near_up) + wide(far_down),
        ]
    ).astype(jnp.bfloat16)
    return attn_out, pool_out


def solution(mesh):
    in_specs = (
        P("pool", "tensor"),
        P("pool", None, "tensor"),
        P("pool", None, None, "tensor"),
        P("tensor", None),
        P("pool", None),
        P("pool", None),
        P("pool"),
        P("pool"),
        P("pool", None),
        P("pool", None),
    )
    out_specs = (P(("pool", "tensor"), None), P("pool", None, None, "tensor"))
    return jax.shard_map(
        on_device, mesh=mesh, in_specs=in_specs, out_specs=out_specs, check_vma=False
    )
```

time: 380 us -> 194 us (0.51)
  Pallas kernels: 228 us -> 70.9 us
  waiting for transfers between devices: 71.1 us -> 57.6 us
  between operations: 15.6 us -> 2.49 us
  starting transfers between devices: 34.7 us -> 43.2 us
  matrix products: 4.95 us -> 0.22 us
  local copies, waits for them, and re-layouts: 16.6 us -> 12.5 us
    pallas_call x4 -> x13, Pallas kernels: 227 us -> 69.4 us  [the longest x4 30 us: attend(): pl.pallas_call(functools.partial(attend_kernel, group=group, tok=tok), ou...]
    all_to_all x4 -> x3, waiting for transfers between devices: 71.1 us -> 56.6 us  [swap_pool(): return lax.all_to_all(x, 'pool', split_axis=0, concat_axis=0, tiled=True)]
    ppermute x0 -> x11, starting transfers between devices: none -> 14.4 us  [the longest x2 5.74 us: on_device(): through_up, through_down = (send_up(up), send_down(down))]
    slice x3 -> x1, local copies, waits for them, and re-layouts: 7.35 us -> 0.97 us  [on_device(): held, _ = lax.optimization_barrier((kv[:, 512:], up))]
    all_to_all x4 -> x3, starting transfers between devices: 34.7 us -> 28.8 us  [swap_pool(): return lax.all_to_all(x, 'pool', split_axis=0, concat_axis=0, tiled=True)]
    dot_general x1 -> x0, matrix products: 4.73 us -> none  [on_device(): jnp.dot(contexts, out_weight, preferred_element_type=jnp.float32)]
    unnamed x20 -> x38, local copies, waits for them, and re-layouts: 5.98 us -> 8.69 us
  transfers between devices with their start and end apart: 5 -> 14, of which waited for: 3 -> 3; matrix products, arithmetic and copies ran while one was open for 5% -> 4% of each run, Pallas kernels for 19% -> 25%
where the time goes in v2:
time: 194 us; the launch traced here: 192 us
  Pallas kernels  70.9 us (37%)
  waiting for transfers between devices  57.6 us (30%)
  starting transfers between devices  43.2 us (22%)
  local copies, waits for them, and re-layouts  12.5 us (6%)
  other arithmetic  4.6 us (2%)
  between operations  2.49 us (1%)
    all_to_all x3, waiting for transfers between devices, swap_pool(): return lax.all_to_all(x, 'pool', split_axis=0, concat_axis=0, tiled=True)  56.6 us
    pallas_call x4, Pallas kernels, attend(): pl.pallas_call(functools.partial(attend_kernel, group=group, tok=tok), ou...  30 us
    all_to_all x3, starting transfers between devices, swap_pool(): return lax.all_to_all(x, 'pool', split_axis=0, concat_axis=0, tiled=True)  28.8 us
    pallas_call x4, Pallas kernels, project(): pl.pallas_call(project_kernel, out_shape=(out, out), in_specs=[VMEM] * (4...  27.6 us
    unnamed x38, local copies, waits for them, and re-layouts  8.69 us
    ppermute x2, starting transfers between devices, on_device(): through_up, through_down = (send_up(up), send_down(down))  5.74 us
    pallas_call x1, Pallas kernels, gather_blocks(): pl.pallas_call(gather_kernel, out_shape=jax.ShapeDtypeStruct((pool, 512 +...  4.33 us
    ppermute x2, starting transfers between devices, on_device(): near_up, near_down = (send_up(up), send_down(down))  4.21 us
  transfers between devices with their start and end apart: 14, of which 3 were waited for; matrix products, arithmetic and copies ran while one was open for 4% of the time, Pallas kernels for 25%

profile of v2, /device:TPU:4, one launch (start us, length us, event | category | flops | bytes accessed | tf_op | source)
XLA Modules:
  0.0 191.5 jit_solution(18105480610421727809)
XLA Ops:
  1.3 1.6 table.1
  2.8 9.0 %all-to-all-start = ((s32[32,1,128]{2,1,0:T(1,128)}), s32[32,1,128]{2,1,0:T(1,128)S(1)}, u32[]{:S(2)}, u32[]{:S(2)}) async-start(s32[32,1,128]{2,1,0:T(1,128)} %get-tuple-element.27), calls=%async_computation | async-start | bytes 32768 | tf_op jit(solution)/shard_map/all_to_all | solution.py:291
  11.8 0.0 copy-start
  11.8 1.6 copy-done
  13.4 1.3 split32.1.pool_ref
  14.7 0.0 copy-start.1
  14.7 1.3 copy-done.1
  16.0 0.7 copy.32
  16.8 1.2 all-to-all-done.wanted
  18.0 0.6 copy-done.9
  18.6 4.3 %gather.1 = bf16[32,544,128]{2,1,0:T(8,128)(2,1)} custom-call(s32[32,1,128]{2,1,0:T(1,128)} %copy-done.9, bf16[32,256,128]{2,1,0:T(8,128)(2,1)} %copy-done.1, bf16[32,32,128]{2,1,0:T(8,128)(2,1)} %bitcast.58), custom_call_target="tpu_custom_call" | custom-call | tf_op jit(solution)/shard_map/gather/pallas_call | solution.py:103
  22.9 7.1 %all-to-all-start.1 = ((bf16[32,544,128]{2,1,0:T(8,128)(2,1)}), bf16[32,544,128]{2,1,0:T(8,128)(2,1)}, u32[]{:S(2)}, u32[]{:S(2)}) async-start(bf16[32,544,128]{2,1,0:T(8,128)(2,1)} %gather.1), calls=%async_computation.1 | async-start | bytes 8912896 | tf_op jit(solution)/shard_map/all_to_all | solution.py:291
  30.1 0.1 collective-permute-start.1
  30.3 0.0 copy-start.7
  30.3 3.0 %copy_pool.1.kept_ref = bf16[32,256,128]{2,1,0:T(8,128)(2,1)} custom-call(bf16[32,256,128]{2,1,0:T(8,128)(2,1)} %bitcast.52), custom_call_target="tpu_custom_call" | custom-call | tf_op jit(solution)/shard_map/copy_pool/pallas_call | solution.py:257
  33.9 0.3 split4.1.new_ref
  34.3 0.1 add_bitcast_fusion.2
  34.4 0.1 add_bitcast_fusion
  34.5 55.4 %all-to-all-done.1.kv_ref = bf16[32,544,128]{2,1,0:T(8,128)(2,1)} async-done(((bf16[32,544,128]{2,1,0:T(8,128)(2,1)}), bf16[32,544,128]{2,1,0:T(8,128)(2,1)}, u32[]{:S(2)}, u32[]{:S(2)}) %all-to-all-start.1) | async-done | bytes 4456480 | tf_op jit(solution)/shard_map/all_to_all | solution.py:291
  89.8 7.4 %attend0.1 = (bf16[64,512]{1,0:T(8,128)(2,1)S(1)}, bf16[64,512]{1,0:T(8,128)(2,1)S(1)}) custom-call(s32[1,64]{1,0:T(1,128)S(1)} %copy-done.8, s32[1]{0:T(128)S(6)} %copy.34.length, s32[4,4]{1,0:T(4,128)S(1)} %pad_add_fusion.base, bf16[512,512]{1,0:T(8,128)(2,1)S(1)} %copy-done.7, bf16[32,544,128]{2,1,0:T(8,128)(2,1)} %all-to-all-done.1.kv_ref, ...), custom_call_target="tpu_custom_call" | custom-call | flops 2281701376 | bytes 5242880 | tf_op jit(solution)/shard_map/attend0/pallas_call | solution.py:205
  97.3 0.6 copy-done.5
  97.9 0.0 collective-permute-start
  97.9 0.1 fusion.5
  98.0 0.1 copy.23
  98.1 0.1 copy.22
  98.2 1.0 collective-permute-done.b_ref
  99.1 0.6 copy-done.15
  99.8 6.9 %project0.3 = (bf16[32,5120]{1,0:T(8,128)(2,1)}, bf16[32,5120]{1,0:T(8,128)(2,1)}) custom-call(bf16[64,512]{1,0:T(8,128)(2,1)} %copy-done.5, bf16[64,512]{1,0:T(8,128)(2,1)} %copy-done.15, bf16[512,5120]{1,0:T(8,128)(2,1)} %wa_ref.7, bf16[512,5120]{1,0:T(8,128)(2,1)} %collective-permute-done.1.wb_ref), custom_call_target="tpu_custom_call" | custom-call | flops 671088640 | bytes 11534336 | tf_op jit(solution)/shard_map/project0/pallas_call | solution.py:237
  106.6 7.4 %attend1.1 = (bf16[64,512]{1,0:T(8,128)(2,1)S(1)}, bf16[64,512]{1,0:T(8,128)(2,1)S(1)}) custom-call(s32[1,64]{1,0:T(1,128)S(1)} %copy-done.8, s32[1]{0:T(128)S(6)} %copy.34.length, s32[4,4]{1,0:T(4,128)S(1)} %pad_add_fusion.base, bf16[512,512]{1,0:T(8,128)(2,1)S(1)} %copy-done.7, bf16[32,544,128]{2,1,0:T(8,128)(2,1)} %all-to-all-done.1.kv_ref, ...), custom_call_target="tpu_custom_call" | custom-call | flops 2281701376 | bytes 5242880 | tf_op jit(solution)/shard_map/attend1/pallas_call | solution.py:205
  114.1 0.6 copy-done.6
  114.7 0.2 collective-permute-start.2
  114.8 0.7 compare_reduce_fusion
  115.6 3.5 %collective-permute-start.4 = (bf16[32,5120]{1,0:T(8,128)(2,1)}, bf16[32,5120]{1,0:T(8,128)(2,1)S(1)}, u32[]{:S(2)}, u32[]{:S(2)}) collective-permute-start(bf16[32,5120]{1,0:T(8,128)(2,1)} %get-tuple-element.30), channel_id=1, source_target_pairs={{0,2},{1,3},{2,4},{3,5},{4,6},{5,7},{6,0},{7,1},{8,10},{9,11},{10,... | collective-permute-start | bytes 983048 | tf_op jit(solution)/shard_map/ppermute | solution.py:343
  119.1 2.2 %collective-permute-start.5 = (bf16[32,5120]{1,0:T(8,128)(2,1)}, bf16[32,5120]{1,0:T(8,128)(2,1)S(1)}, u32[]{:S(2)}, u32[]{:S(2)}) collective-permute-start(bf16[32,5120]{1,0:T(8,128)(2,1)} %get-tuple-element.38), channel_id=1, source_target_pairs={{2,0},{3,1},{4,2},{5,3},{6,4},{7,5},{0,6},{1,7},{10,8},{11,9},{12,... | collective-permute-start | bytes 983048 | tf_op jit(solution)/shard_map/ppermute | solution.py:343
  121.3 0.6 copy-done.16
  121.9 6.9 %project0.4 = (bf16[32,5120]{1,0:T(8,128)(2,1)}, bf16[32,5120]{1,0:T(8,128)(2,1)}) custom-call(bf16[64,512]{1,0:T(8,128)(2,1)} %copy-done.6, bf16[64,512]{1,0:T(8,128)(2,1)} %copy-done.16, bf16[512,5120]{1,0:T(8,128)(2,1)} %wa_ref.7, bf16[512,5120]{1,0:T(8,128)(2,1)} %collective-permute-done.1.wb_ref), custom_call_target="tpu_custom_call" | custom-call | flops 671088640 | bytes 11534336 | tf_op jit(solution)/shard_map/project0/pallas_call | solution.py:237
  128.8 7.5 %attend2.1 = (bf16[64,512]{1,0:T(8,128)(2,1)S(1)}, bf16[64,512]{1,0:T(8,128)(2,1)S(1)}) custom-call(s32[1,64]{1,0:T(1,128)S(1)} %copy-done.8, s32[1]{0:T(128)S(6)} %copy.34.length, s32[4,4]{1,0:T(4,128)S(1)} %pad_add_fusion.base, bf16[512,512]{1,0:T(8,128)(2,1)S(1)} %copy-done.7, bf16[32,544,128]{2,1,0:T(8,128)(2,1)} %all-to-all-done.1.kv_ref, ...), custom_call_target="tpu_custom_call" | custom-call | flops 2281701376 | bytes 5242880 | tf_op jit(solution)/shard_map/attend2/pallas_call | solution.py:205
  136.3 0.6 copy-done.3
  137.0 0.1 collective-permute-start.3
  137.0 0.6 fusion.3.slots
  137.6 1.0 slice.19
  138.6 1.4 collective-permute-start.9
  140.1 2.8 %collective-permute-start.8 = (bf16[32,5120]{1,0:T(8,128)(2,1)S(1)}, bf16[32,5120]{1,0:T(8,128)(2,1)S(1)}, u32[]{:S(2)}, u32[]{:S(2)}) collective-permute-start(bf16[32,5120]{1,0:T(8,128)(2,1)S(1)} %copy-done.17), channel_id=1, source_target_pairs={{2,0},{3,1},{4,2},{5,3},{6,4},{7,5},{0,6},{1,7},{10,8},{11,9},{12,... | collective-permute-start | bytes 983048 | tf_op jit(solution)/shard_map/ppermute | solution.py:345
  142.9 0.0 copy-start.11
  142.9 0.6 copy-done.13
  143.5 0.1 copy-done.11
  143.6 0.1 copy-done.12
  143.7 7.0 %project2.1 = (bf16[32,5120]{1,0:T(8,128)(2,1)}, bf16[32,5120]{1,0:T(8,128)(2,1)}) custom-call(bf16[64,512]{1,0:T(8,128)(2,1)} %copy-done.3, bf16[64,512]{1,0:T(8,128)(2,1)} %copy-done.13, bf16[512,5120]{1,0:T(8,128)(2,1)} %wa_ref.7, bf16[512,5120]{1,0:T(8,128)(2,1)} %collective-permute-done.1.wb_ref, bf16[32,5120]{1,0:T(8,128)(2,1)} %copy-done.11, ...), custom_call_target="tpu_custom_call" | custom-call | flops 671088640 | bytes 11534336 | tf_op jit(solution)/shard_map/project2/pallas_call | solution.py:237
  150.7 1.3 collective-permute-start.7
  152.0 2.8 %collective-permute-start.10 = (bf16[32,5120]{1,0:T(8,128)(2,1)}, bf16[32,5120]{1,0:T(8,128)(2,1)S(1)}, u32[]{:S(2)}, u32[]{:S(2)}) collective-permute-start(bf16[32,5120]{1,0:T(8,128)(2,1)} %get-tuple-element.46), channel_id=1, source_target_pairs={{2,0},{3,1},{4,2},{5,3},{6,4},{7,5},{0,6},{1,7},{10,8},{11,9},{12,... | collective-permute-start | bytes 983048 | tf_op jit(solution)/shard_map/ppermute | solution.py:347
  154.8 7.6 %attend3.1 = (bf16[64,512]{1,0:T(8,128)(2,1)S(1)}, bf16[64,512]{1,0:T(8,128)(2,1)S(1)}) custom-call(s32[1,64]{1,0:T(1,128)S(1)} %copy-done.8, s32[1]{0:T(128)S(6)} %copy.34.length, s32[4,4]{1,0:T(4,128)S(1)} %pad_add_fusion.base, bf16[512,512]{1,0:T(8,128)(2,1)S(1)} %copy-done.7, bf16[32,544,128]{2,1,0:T(8,128)(2,1)} %all-to-all-done.1.kv_ref, ...), custom_call_target="tpu_custom_call" | custom-call | flops 2281701376 | bytes 5242880 | tf_op jit(solution)/shard_map/attend3/pallas_call | solution.py:205
  162.4 0.6 copy-done.4
  163.1 0.1 reshape.43
  163.1 0.2 fusion
  163.4 0.9 copy.25
  164.3 12.7 %all-to-all-start.2 = ((bf16[32,4,1024]{2,1,0:T(4,128)(2,1)}), bf16[32,4,1024]{2,1,0:T(4,128)(2,1)S(1)}, u32[]{:S(2)}, u32[]{:S(2)}) async-start(bf16[32,4,1024]{2,1,0:T(4,128)(2,1)} %copy.25), calls=%async_computation.2 | async-start | bytes 524288 | tf_op jit(solution)/shard_map/all_to_all | solution.py:291
  177.0 0.6 copy-done.14
  177.6 6.9 %project0.5 = (bf16[32,5120]{1,0:T(8,128)(2,1)}, bf16[32,5120]{1,0:T(8,128)(2,1)}) custom-call(bf16[64,512]{1,0:T(8,128)(2,1)} %copy-done.4, bf16[64,512]{1,0:T(8,128)(2,1)} %copy-done.14, bf16[512,5120]{1,0:T(8,128)(2,1)} %wa_ref.7, bf16[512,5120]{1,0:T(8,128)(2,1)} %collective-permute-done.1.wb_ref), custom_call_target="tpu_custom_call" | custom-call | flops 671088640 | bytes 11534336 | tf_op jit(solution)/shard_map/project0/pallas_call | solution.py:237
  184.5 1.1 add_convert_fusion
  185.6 1.1 add_convert_fusion.1
  186.7 0.9 pad_maximum_fusion
  187.6 0.1 reshape.44
  187.7 0.7 copy.31
  188.5 2.9 %write.1 = bf16[32,256,128]{2,1,0:T(8,128)(2,1)} custom-call(s32[4]{0:T(128)} %fusion.3.slots, bf16[4,256,128]{2,1,0:T(8,128)(2,1)} %bitcast.57, bf16[32,256,128]{2,1,0:T(8,128)(2,1)} %copy_pool.1.kept_ref), custom_call_target="tpu_custom_call", output_to_operand_aliasing={{}: (2, {})} | custom-call | tf_op jit(solution)/shard_map/write/pallas_call | solution.py:279
  (34 shorter events, 0.1 us)
Async XLA Ops:
  2.8 15.2 %all-to-all-start = ((s32[32,1,128]{2,1,0:T(1,128)}), s32[32,1,128]{2,1,0:T(1,128)S(1)}, u32[]{:S(2)}, u32[]{:S(2)}) async-start(s32[32,1,128]{2,1,0:T(1,128)} %get-tuple-element.27), calls=%async_computation | async-start | bytes 32768 | tf_op jit(solution)/shard_map/all_to_all | solution.py:291
  11.8 1.6 copy-start
  13.4 2.6 %copy-start.2 = (bf16[512,2,128]{2,1,0:T(2,128)(2,1)S(1)}, bf16[512,2,128]{2,1,0:T(2,128)(2,1)}, u32[]{:S(2)}) copy-start(bf16[512,2,128]{2,1,0:T(2,128)(2,1)} %param.11) | copy-start | bytes 786436
  14.7 1.3 copy-start.1
  18.0 0.6 copy-start.9
  22.9 66.9 %all-to-all-start.1 = ((bf16[32,544,128]{2,1,0:T(8,128)(2,1)}), bf16[32,544,128]{2,1,0:T(8,128)(2,1)}, u32[]{:S(2)}, u32[]{:S(2)}) async-start(bf16[32,544,128]{2,1,0:T(8,128)(2,1)} %gather.1), calls=%async_computation.1 | async-start | bytes 8912896 | tf_op jit(solution)/shard_map/all_to_all | solution.py:291
  30.1 68.1 %collective-permute-start.1 = (bf16[512,5120]{1,0:T(8,128)(2,1)}, bf16[512,5120]{1,0:T(8,128)(2,1)}, u32[]{:S(2)}, u32[]{:S(2)}) collective-permute-start(bf16[512,5120]{1,0:T(8,128)(2,1)} %wa_ref.7), channel_id=1, source_target_pairs={{0,1},{1,0},{2,3},{3,2},{4,5},{5,4},{6,7},{7,6},{8,9},{9,8},{10,11... | collective-permute-start | bytes 15728648 | tf_op jit(solution)/shard_map/ppermute | solution.py:334
  30.3 59.6 %copy-start.7 = (bf16[512,512]{1,0:T(8,128)(2,1)S(1)}, bf16[512,512]{1,0:T(8,128)(2,1)}, u32[]{:S(2)}) copy-start(bf16[512,512]{1,0:T(8,128)(2,1)} %q_ref.7) | copy-start | bytes 1572868
  30.3 59.5 %copy-start.8 = (s32[1,64]{1,0:T(1,128)S(1)}, s32[1,64]{1,0:T(1,128)}, u32[]{:S(2)}) copy-start(s32[1,64]{1,0:T(1,128)} %get-tuple-element.40.order) | copy-start | bytes 772
  34.4 63.5 %copy-start.10 = (s32[32,1,128]{2,1,0:T(1,128)S(1)}, s32[32,1,128]{2,1,0:T(1,128)}, u32[]{:S(2)}) copy-start(s32[32,1,128]{2,1,0:T(1,128)} %copy-done.9) | copy-start | bytes 49156
  97.3 0.6 copy-start.5
  97.9 1.3 collective-permute-start
  99.1 0.6 copy-start.15
  114.1 0.6 copy-start.6
  114.7 6.6 %collective-permute-start.2 = (bf16[64,512]{1,0:T(8,128)(2,1)S(1)}, bf16[64,512]{1,0:T(8,128)(2,1)S(1)}, u32[]{:S(2)}, u32[]{:S(2)}) collective-permute-start(bf16[64,512]{1,0:T(8,128)(2,1)S(1)} %get-tuple-element.33), channel_id=1, source_target_pairs={{0,1},{1,0},{2,3},{3,2},{4,5},{5,4},{6,7},{7,6},{8,9},{9,8},{10,11... | collective-permute-start | bytes 196616 | tf_op jit(solution)/shard_map/ppermute | solution.py:340
  115.6 27.3 %collective-permute-start.4 = (bf16[32,5120]{1,0:T(8,128)(2,1)}, bf16[32,5120]{1,0:T(8,128)(2,1)S(1)}, u32[]{:S(2)}, u32[]{:S(2)}) collective-permute-start(bf16[32,5120]{1,0:T(8,128)(2,1)} %get-tuple-element.30), channel_id=1, source_target_pairs={{0,2},{1,3},{2,4},{3,5},{4,6},{5,7},{6,0},{7,1},{8,10},{9,11},{10,... | collective-permute-start | bytes 983048 | tf_op jit(solution)/shard_map/ppermute | solution.py:343
  119.1 23.8 %collective-permute-start.5 = (bf16[32,5120]{1,0:T(8,128)(2,1)}, bf16[32,5120]{1,0:T(8,128)(2,1)S(1)}, u32[]{:S(2)}, u32[]{:S(2)}) collective-permute-start(bf16[32,5120]{1,0:T(8,128)(2,1)} %get-tuple-element.38), channel_id=1, source_target_pairs={{2,0},{3,1},{4,2},{5,3},{6,4},{7,5},{0,6},{1,7},{10,8},{11,9},{12,... | collective-permute-start | bytes 983048 | tf_op jit(solution)/shard_map/ppermute | solution.py:343
  121.3 0.6 copy-start.16
  128.8 9.8 %copy-start.18 = (bf16[32,5120]{1,0:T(8,128)(2,1)S(1)}, bf16[32,5120]{1,0:T(8,128)(2,1)}, u32[]{:S(2)}) copy-start(bf16[32,5120]{1,0:T(8,128)(2,1)} %get-tuple-element.34) | copy-start | bytes 983044
  128.8 11.3 %copy-start.17 = (bf16[32,5120]{1,0:T(8,128)(2,1)S(1)}, bf16[32,5120]{1,0:T(8,128)(2,1)}, u32[]{:S(2)}) copy-start(bf16[32,5120]{1,0:T(8,128)(2,1)} %get-tuple-element.44) | copy-start | bytes 983044
  136.3 0.6 copy-start.3
  137.0 5.9 %collective-permute-start.3 = (bf16[64,512]{1,0:T(8,128)(2,1)S(1)}, bf16[64,512]{1,0:T(8,128)(2,1)S(1)}, u32[]{:S(2)}, u32[]{:S(2)}) collective-permute-start(bf16[64,512]{1,0:T(8,128)(2,1)S(1)} %get-tuple-element.37), channel_id=1, source_target_pairs={{0,1},{1,0},{2,3},{3,2},{4,5},{5,4},{6,7},{7,6},{8,9},{9,8},{10,11... | collective-permute-start | bytes 196616 | tf_op jit(solution)/shard_map/ppermute | solution.py:340
  138.6 45.9 %collective-permute-start.9 = (bf16[32,5120]{1,0:T(8,128)(2,1)S(1)}, bf16[32,5120]{1,0:T(8,128)(2,1)S(1)}, u32[]{:S(2)}, u32[]{:S(2)}) collective-permute-start(bf16[32,5120]{1,0:T(8,128)(2,1)S(1)} %copy-done.18), channel_id=1, source_target_pairs={{0,2},{1,3},{2,4},{3,5},{4,6},{5,7},{6,0},{7,1},{8,10},{9,11},{10,... | collective-permute-start | bytes 983048 | tf_op jit(solution)/shard_map/ppermute | solution.py:345
  140.1 45.5 %collective-permute-start.8 = (bf16[32,5120]{1,0:T(8,128)(2,1)S(1)}, bf16[32,5120]{1,0:T(8,128)(2,1)S(1)}, u32[]{:S(2)}, u32[]{:S(2)}) collective-permute-start(bf16[32,5120]{1,0:T(8,128)(2,1)S(1)} %copy-done.17), channel_id=1, source_target_pairs={{2,0},{3,1},{4,2},{5,3},{6,4},{7,5},{0,6},{1,7},{10,8},{11,9},{12,... | collective-permute-start | bytes 983048 | tf_op jit(solution)/shard_map/ppermute | solution.py:345
  142.9 0.6 copy-start.13
  142.9 0.7 copy-start.11
  142.9 0.8 copy-start.12
  150.7 35.0 %collective-permute-start.7 = (bf16[32,5120]{1,0:T(8,128)(2,1)}, bf16[32,5120]{1,0:T(8,128)(2,1)S(1)}, u32[]{:S(2)}, u32[]{:S(2)}) collective-permute-start(bf16[32,5120]{1,0:T(8,128)(2,1)} %get-tuple-element.39), channel_id=1, source_target_pairs={{0,2},{1,3},{2,4},{3,5},{4,6},{5,7},{6,0},{7,1},{8,10},{9,11},{10,... | collective-permute-start | bytes 983048 | tf_op jit(solution)/shard_map/ppermute | solution.py:347
  152.0 32.5 %collective-permute-start.10 = (bf16[32,5120]{1,0:T(8,128)(2,1)}, bf16[32,5120]{1,0:T(8,128)(2,1)S(1)}, u32[]{:S(2)}, u32[]{:S(2)}) collective-permute-start(bf16[32,5120]{1,0:T(8,128)(2,1)} %get-tuple-element.46), channel_id=1, source_target_pairs={{2,0},{3,1},{4,2},{5,3},{6,4},{7,5},{0,6},{1,7},{10,8},{11,9},{12,... | collective-permute-start | bytes 983048 | tf_op jit(solution)/shard_map/ppermute | solution.py:347
  162.4 0.6 copy-start.4
  163.1 14.0 %collective-permute-start.6 = (bf16[64,512]{1,0:T(8,128)(2,1)S(1)}, bf16[64,512]{1,0:T(8,128)(2,1)S(1)}, u32[]{:S(2)}, u32[]{:S(2)}) collective-permute-start(bf16[64,512]{1,0:T(8,128)(2,1)S(1)} %get-tuple-element.42), channel_id=1, source_target_pairs={{0,1},{1,0},{2,3},{3,2},{4,5},{5,4},{6,7},{7,6},{8,9},{9,8},{10,11... | collective-permute-start | bytes 196616 | tf_op jit(solution)/shard_map/ppermute | solution.py:340
  164.3 23.3 %all-to-all-start.2 = ((bf16[32,4,1024]{2,1,0:T(4,128)(2,1)}), bf16[32,4,1024]{2,1,0:T(4,128)(2,1)S(1)}, u32[]{:S(2)}, u32[]{:S(2)}) async-start(bf16[32,4,1024]{2,1,0:T(4,128)(2,1)} %copy.25), calls=%async_computation.2 | async-start | bytes 524288 | tf_op jit(solution)/shard_map/all_to_all | solution.py:291
  177.0 0.6 copy-start.14

commit v3 on v2

--- a/solution.py
+++ b/solution.py
@@ -14,9 +14,16 @@
 SMEM = pl.BlockSpec(memory_space=pltpu.SMEM)
 VMEM = pl.BlockSpec(memory_space=pltpu.VMEM)
 ANY = pl.BlockSpec(memory_space=pl.ANY)
-
-
-def meta_kernel(dest_owner, dest_slot, evict, owner_ref, block_ref, meta_ref, order_ref):
+HBM = pl.BlockSpec(memory_space=pltpu.HBM)
+
+
+def limit(mebibytes):
+    return pltpu.CompilerParams(vmem_limit_bytes=mebibytes * 2**20)
+
+
+def meta_kernel(
+    dest_owner, dest_slot, evict, owner_ref, block_ref, pieces_ref, meta_ref, order_ref
+):
     pool, entries = meta_ref.shape[0], owner_ref.shape[1]
     owner = jnp.broadcast_to(owner_ref[...], (pool, entries))
     block = jnp.broadcast_to(block_ref[...], (pool, entries))
@@ -35,20 +42,25 @@
         out = jnp.where(lane == 6 + b, dest_slot[0, b], out)
     out = jnp.where(lane == 10, evict[0], out)
     for o in range(pool):
-        meta_ref[o] = out[o : o + 1]
-
-
-def exchange_table(hist_owner, hist_block, dest_owner, dest_slot, evict, pool):
+        meta_ref[o, 0 : pieces_ref.shape[1], :] = pieces_ref[o]
+        meta_ref[o, pieces_ref.shape[1] :, :] = jnp.broadcast_to(
+            out[o : o + 1].astype(jnp.float32), (16, 128)
+        ).astype(jnp.bfloat16)
+
+
+def exchange_table(hist_owner, hist_block, dest_owner, dest_slot, evict, pieces):
+    pool, rows, _ = pieces.shape
     return pl.pallas_call(
         meta_kernel,
         out_shape=(
-            jax.ShapeDtypeStruct((pool, 1, 128), jnp.int32),
+            jax.ShapeDtypeStruct((pool, rows + 16, 128), jnp.bfloat16),
             jax.ShapeDtypeStruct(hist_owner.shape, jnp.int32),
         ),
-        in_specs=[SMEM, SMEM, SMEM, VMEM, VMEM],
+        in_specs=[SMEM, SMEM, SMEM, VMEM, VMEM, VMEM],
         out_specs=(VMEM, VMEM),
+        compiler_params=limit(4),
         name="table",
-    )(dest_owner, dest_slot, evict, hist_owner, hist_block)
+    )(dest_owner, dest_slot, evict, hist_owner, hist_block, pieces)
 
 
 def split_kernel(x_ref, o_ref):
@@ -70,49 +82,58 @@
         out_shape=jax.ShapeDtypeStruct(x.shape, x.dtype),
         in_specs=[VMEM],
         out_specs=VMEM,
-        compiler_params=pltpu.CompilerParams(vmem_limit_bytes=12 * 2**20),
+        compiler_params=limit(12),
         name=f"split{x.shape[0]}",
     )(x)
 
 
-def gather_kernel(wanted, pool_ref, pieces_ref, out_ref, sems):
+def gather_kernel(told, pool_ref, held_ref, out_ref, held, onward, packed, sems):
+    pool, rows = packed.shape[:2]
     copies = []
-    pool = out_ref.shape[0]
     for p in range(pool):
         for r in range(2):
             copies.append(
                 pltpu.make_async_copy(
-                    pool_ref.at[wanted[p, 0, r]],
-                    out_ref.at[p, pl.ds(256 * r, 256)],
-                    sems.at[2 * p + r],
+                    pool_ref.at[told[p, r]], out_ref.at[p, pl.ds(256 * r, 256)], sems.at[2 * p + r]
                 )
             )
             copies[-1].start()
+    held[...] = held_ref[...].astype(jnp.float32)
+    for b in range(4):
+        for p in range(pool):
+            onward[told[p, 2 + b], 8 * b : 8 * b + 8, :] = held[p, 8 * b : 8 * b + 8, :]
+    packed[...] = onward[...].astype(jnp.bfloat16)
     copies.append(
-        pltpu.make_async_copy(
-            pieces_ref, out_ref.at[:, pl.ds(512, pieces_ref.shape[1])], sems.at[2 * pool]
-        )
+        pltpu.make_async_copy(packed, out_ref.at[:, pl.ds(512, rows)], sems.at[2 * pool])
     )
     copies[-1].start()
     for copy in copies:
         copy.wait()
 
 
-def gather_blocks(wanted, pool_blocks, pieces):
-    pool = wanted.shape[0]
+def gather_blocks(told, pool_blocks, held):
+    pool, rows, _ = held.shape
     return pl.pallas_call(
         gather_kernel,
-        out_shape=jax.ShapeDtypeStruct((pool, 512 + pieces.shape[1], 128), pool_blocks.dtype),
+        out_shape=jax.ShapeDtypeStruct((pool, 512 + rows, 128), pool_blocks.dtype),
         in_specs=[SMEM, VMEM, VMEM],
-        out_specs=ANY,
-        scratch_shapes=[pltpu.SemaphoreType.DMA((2 * pool + 1,))],
+        out_specs=HBM,
+        scratch_shapes=[
+            pltpu.VMEM(held.shape, jnp.float32),
+            pltpu.VMEM(held.shape, jnp.float32),
+            pltpu.VMEM(held.shape, jnp.bfloat16),
+            pltpu.SemaphoreType.DMA((2 * pool + 1,)),
+        ],
+        compiler_params=limit(51),
         name="gather",
-    )(wanted, pool_blocks, pieces)
+    )(told, pool_blocks, held)
 
 
 def attend_kernel(
-    order, length, base, q_ref, kv_ref, new_ref, mine_ref, theirs_ref, sbuf, *, group, tok
+    order, length, base, q_ref, new_ref, kv_any, mine_ref, theirs_ref, sbuf, kv_ref, sem, *, group, tok
 ):
+    fetch = pltpu.make_async_copy(kv_any.at[:, pl.ds(0, kv_ref.shape[1])], kv_ref, sem)
+    fetch.start()
     c = math.log2(math.e) / math.sqrt(HEAD)
     heads = q_ref.shape[1] // HEAD
     rows = heads * tok
@@ -173,6 +194,7 @@
     n = length[0]
     full = n // CHUNK
     last = order.shape[1] // CHUNK - 1
+    fetch.wait()
     sbuf[0] = scores(keys_of(0))
 
     def step(i, state, a):
@@ -205,23 +227,41 @@
     return pl.pallas_call(
         functools.partial(attend_kernel, group=group, tok=tok),
         out_shape=(out, out),
-        in_specs=[SMEM, SMEM, SMEM, VMEM, VMEM, VMEM],
+        in_specs=[SMEM, SMEM, SMEM, VMEM, VMEM, HBM],
         out_specs=(VMEM, VMEM),
-        scratch_shapes=[pltpu.VMEM((2, CHUNK * 128, heads * tok), jnp.float32)],
-        compiler_params=pltpu.CompilerParams(vmem_limit_bytes=16 * 2**20),
-        cost_estimate=pl.CostEstimate(
-            flops=tok * heads * 8704 * 128 * 4, bytes_accessed=5 * 2**20, transcendentals=0
-        ),
+        scratch_shapes=[
+            pltpu.VMEM((2, CHUNK * 128, heads * tok), jnp.float32),
+            pltpu.VMEM((kv.shape[0], 512, 128), kv.dtype),
+            pltpu.SemaphoreType.DMA,
+        ],
+        compiler_params=limit(16),
         name=f"attend{group}",
-    )(order, length, base, queries, kv, fresh)
-
-
-def project_kernel(a_ref, b_ref, wa_ref, wb_ref, *refs):
-    arrived, (up_ref, down_ref) = refs[:-2], refs[-2:]
+    )(order, length, base, queries, fresh, kv)
+
+
+def project_kernel(a_ref, b_ref, *refs, arriving):
+    arrived, (wa_any, wb_any, up_ref, down_ref, wa_ref, wb_ref, sems) = (
+        refs[:arriving],
+        refs[arriving:],
+    )
     half = a_ref.shape[0] // 2
-    tile = 512
-    for j in range(wa_ref.shape[1] // tile):
+    tiles = sems.shape[0]
+    tile = wa_ref.shape[1] // tiles
+    copies = []
+    for j in range(tiles):
+        cols = pl.ds(j * tile, tile)
+        copies.append(
+            (
+                pltpu.make_async_copy(wa_any.at[:, cols], wa_ref.at[:, cols], sems.at[j, 0]),
+                pltpu.make_async_copy(wb_any.at[:, cols], wb_ref.at[:, cols], sems.at[j, 1]),
+            )
+        )
+        for copy in copies[-1]:
+            copy.start()
+    for j in range(tiles):
         cols = slice(j * tile, (j + 1) * tile)
+        for copy in copies[j]:
+            copy.wait()
         total = jnp.dot(a_ref[...], wa_ref[:, cols], preferred_element_type=jnp.float32)
         total += jnp.dot(b_ref[...], wb_ref[:, cols], preferred_element_type=jnp.float32)
         up, down = total[:half], total[half:]
@@ -235,15 +275,37 @@
 def project(a, b, wa, wb, *arrived):
     out = jax.ShapeDtypeStruct((a.shape[0] // 2, wa.shape[1]), jnp.bfloat16)
     return pl.pallas_call(
-        project_kernel,
+        functools.partial(project_kernel, arriving=len(arrived)),
         out_shape=(out, out),
-        in_specs=[VMEM] * (4 + len(arrived)),
+        in_specs=[VMEM] * (2 + len(arrived)) + [HBM, HBM],
         out_specs=(VMEM, VMEM),
-        cost_estimate=pl.CostEstimate(
-            flops=4 * a.size * wa.shape[1], bytes_accessed=11 * 2**20, transcendentals=0
-        ),
+        scratch_shapes=[
+            pltpu.VMEM(wa.shape, wa.dtype),
+            pltpu.VMEM(wb.shape, wb.dtype),
+            pltpu.SemaphoreType.DMA((10, 2)),
+        ],
+        compiler_params=limit(52),
         name=f"project{len(arrived)}",
-    )(a, b, wa, wb, *arrived)
+    )(a, b, *arrived, wa, wb)
+
+
+def combine_kernel(top, bottom, far_up, near_down, near_up, far_down, o_ref):
+    half = top.shape[0]
+    for rows, parts in ((0, (top, far_up, near_down)), (half, (bottom, near_up, far_down))):
+        total = sum(part[...].astype(jnp.float32) for part in parts)
+        o_ref[rows : rows + half, :] = total.astype(jnp.bfloat16)
+
+
+def combine(*parts):
+    rows, width = parts[0].shape
+    return pl.pallas_call(
+        combine_kernel,
+        out_shape=jax.ShapeDtypeStruct((2 * rows, width), jnp.bfloat16),
+        in_specs=[VMEM] * 6,
+        out_specs=VMEM,
+        compiler_params=limit(8),
+        name="combine",
+    )(*parts)
 
 
 def copy_kernel(x_ref, o_ref, buf, sem):
@@ -257,9 +319,10 @@
     return pl.pallas_call(
         copy_kernel,
         out_shape=jax.ShapeDtypeStruct(x.shape, x.dtype),
-        in_specs=[ANY],
-        out_specs=ANY,
+        in_specs=[HBM],
+        out_specs=HBM,
         scratch_shapes=[pltpu.VMEM(x.shape, x.dtype), pltpu.SemaphoreType.DMA],
+        compiler_params=limit(4),
         name="copy_pool",
     )(x)
 
@@ -283,6 +346,7 @@
         out_specs=ANY,
         input_output_aliases={2: 0},
         scratch_shapes=[pltpu.SemaphoreType.DMA((fresh.shape[0],))],
+        compiler_params=limit(4),
         name="write",
     )(slots, fresh, kept)
 
@@ -325,12 +389,13 @@
         ]
     ).astype(jnp.int32)
 
-    table, order = exchange_table(hist_owner, hist_block, dest_owner, dest_slot, evict, pool)
-    told = swap_pool(table)
+    pieces = new_key_value.reshape(4, pool, 8, 128).transpose(1, 0, 2, 3).reshape(pool, 32, 128)
+    table, order = exchange_table(hist_owner, hist_block, dest_owner, dest_slot, evict, pieces)
+    arrived = swap_pool(table)
     pool_blocks = split_blocks(saved.reshape(-1, 256, 128))
     fresh = split_blocks(new_key_value.reshape(-1, 256, 128))
-    pieces = new_key_value.reshape(4, pool, 8, 128).transpose(1, 0, 2, 3).reshape(pool, 32, 128)
-    kv = swap_pool(gather_blocks(told, pool_blocks, pieces))
+    told = arrived[:, 32, :].astype(jnp.int32)
+    kv = swap_pool(gather_blocks(told, pool_blocks, arrived[:, :32]))
     other_weight = swap(out_weight)
     kept = copy_pool(saved.reshape(-1, 256, 128))
 
@@ -339,33 +404,19 @@
         mine, theirs = attend(queries, kv, fresh, first, hist_len, base, group)
         return mine, swap(theirs)
 
-    up, down = project(*contexts(0, order), out_weight, other_weight)
+    up, down = project(*contexts(0, kept), out_weight, other_weight)
     through_up, through_down = send_up(up), send_down(down)
     up, down = project(*contexts(1, up), out_weight, other_weight)
     near_up, near_down = send_up(up), send_down(down)
     up, down = project(*contexts(2, up), out_weight, other_weight, through_up, through_down)
     far_up, far_down = send_up(up), send_down(down)
 
-    held, _ = lax.optimization_barrier((kv[:, 512:], up))
-    held = held.reshape(pool, 4, -1)
-    targets = told[:, 0, 2:6]
-    chosen = targets.T[:, None, :] == jnp.arange(pool, dtype=jnp.int32)[None, :, None]
-    onward = jnp.einsum(
-        "bop,pbx->obx", chosen.astype(jnp.bfloat16), held, preferred_element_type=jnp.float32
-    ).astype(jnp.bfloat16)
-    returned = swap_pool(onward).reshape(pool, 4, 8, 128).transpose(1, 0, 2, 3)
-    mine = (targets == me) & (told[:, 0, 10:11] > 0)
-    slots = jnp.max(jnp.where(mine, told[:, 0, 6:10], -1), axis=0)
-
-    top, bottom = project(*contexts(3, up), out_weight, other_weight)
+    returned = kv[:, 512:].reshape(pool, 4, 8, 128).transpose(1, 0, 2, 3)
+    mine = (told[:, 2:6] == me) & (told[:, 10:11] > 0)
+    slots = jnp.max(jnp.where(mine, told[:, 6:10], -1), axis=0)
+    top, bottom = project(*contexts(3, (near_up, near_down)), out_weight, other_weight)
     pool_out = write_back(slots, returned.reshape(4, 256, 128), kept).reshape(saved.shape)
-    wide = lambda x: x.astype(jnp.float32)
-    attn_out = jnp.concatenate(
-        [
-            wide(top) + wide(far_up) + wide(near_down),
-            wide(bottom) + wide(near_up) + wide(far_down),
-        ]
-    ).astype(jnp.bfloat16)
+    attn_out = combine(top, bottom, far_up, near_down, near_up, far_down)
     return attn_out, pool_out
 
 

time: 194 us -> 178 us (0.918)
  starting transfers between devices: 43.2 us -> 30.2 us
  local copies, waits for them, and re-layouts: 12.5 us -> 6.24 us
  waiting for transfers between devices: 57.6 us -> 63.5 us
  other arithmetic: 4.6 us -> 0.46 us
    all_to_all x3 -> x2, starting transfers between devices: 28.8 us -> 15.7 us  [swap_pool(): return lax.all_to_all(x, 'pool', split_axis=0, concat_axis=0, tiled=True)]
    pallas_call x4, Pallas kernels: 30 us -> 41.7 us  [attend(): pl.pallas_call(functools.partial(attend_kernel, group=group, tok=tok), ou...]
    pallas_call x5 -> x6, Pallas kernels: 29.1 us -> 22.2 us  [the longest x4 19.5 us: project(): pl.pallas_call(functools.partial(project_kernel, arriving=len(arrived)),...]
    unnamed x38 -> x16, local copies, waits for them, and re-layouts: 8.69 us -> 4.22 us
    all_to_all x3 -> x2, waiting for transfers between devices: 56.6 us -> 60 us  [swap_pool(): return lax.all_to_all(x, 'pool', split_axis=0, concat_axis=0, tiled=True)]
    ppermute x4, waiting for transfers between devices: 0.97 us -> 3.53 us  [contexts(): return (mine, swap(theirs))]
    another operation x2 -> x0, other arithmetic: 2.19 us -> none
  transfers between devices with their start and end apart: 14 -> 13, of which waited for: 3 -> 5; matrix products, arithmetic and copies ran while one was open for 4% -> 1% of each run, Pallas kernels for 25% -> 35%
where the time goes in v3:
time: 178 us; the launch traced here: 175 us
  Pallas kernels  72.4 us (41%)
  waiting for transfers between devices  63.5 us (36%)
  starting transfers between devices  30.2 us (17%)
  local copies, waits for them, and re-layouts  6.24 us (4%)
  between operations  2.3 us (1%)
    all_to_all x2, waiting for transfers between devices, swap_pool(): return lax.all_to_all(x, 'pool', split_axis=0, concat_axis=0, tiled=True)  60 us
    pallas_call x4, Pallas kernels, attend(): pl.pallas_call(functools.partial(attend_kernel, group=group, tok=tok), ou...  41.7 us
    pallas_call x4, Pallas kernels, project(): pl.pallas_call(functools.partial(project_kernel, arriving=len(arrived)),...  19.5 us
    all_to_all x2, starting transfers between devices, swap_pool(): return lax.all_to_all(x, 'pool', split_axis=0, concat_axis=0, tiled=True)  15.7 us
    ppermute x2, starting transfers between devices, on_device(): through_up, through_down = (send_up(up), send_down(down))  5.48 us
    ppermute x2, starting transfers between devices, on_device(): far_up, far_down = (send_up(up), send_down(down))  4.31 us
    unnamed x16, local copies, waits for them, and re-layouts  4.22 us
    ppermute x2, starting transfers between devices, on_device(): near_up, near_down = (send_up(up), send_down(down))  4.22 us
  transfers between devices with their start and end apart: 13, of which 5 were waited for; matrix products, arithmetic and copies ran while one was open for 1% of the time, Pallas kernels for 35%

profile of v3, /device:TPU:4, one launch (start us, length us, event | category | flops | bytes accessed | tf_op | source)
XLA Modules:
  0.0 175.1 jit_solution(12907404904162075171)
XLA Ops:
  1.3 1.0 copy.19
  2.3 0.0 copy-start.4
  2.3 0.6 copy-done.4
  2.9 0.0 copy-start.5
  2.9 0.7 copy-done.5
  3.6 0.0 copy-start.6
  3.6 0.7 copy-done.6
  4.2 0.0 copy-start.7
  4.2 0.7 copy-done.7
  4.9 1.6 table.1
  6.5 9.0 %all-to-all-start = ((bf16[32,48,128]{2,1,0:T(8,128)(2,1)}), bf16[32,48,128]{2,1,0:T(8,128)(2,1)S(1)}, u32[]{:S(2)}, u32[]{:S(2)}) async-start(bf16[32,48,128]{2,1,0:T(8,128)(2,1)} %get-tuple-element.26), calls=%async_computation | async-start | bytes 786432 | tf_op jit(solution)/shard_map/all_to_all | solution.py:355
  15.4 0.0 copy-start
  15.4 1.6 copy-done
  17.0 1.3 split32.1.pool_ref
  18.3 5.6 %all-to-all-done = bf16[32,48,128]{2,1,0:T(8,128)(2,1)S(1)} async-done(((bf16[32,48,128]{2,1,0:T(8,128)(2,1)}), bf16[32,48,128]{2,1,0:T(8,128)(2,1)S(1)}, u32[]{:S(2)}, u32[]{:S(2)}) %all-to-all-start) | async-done | bytes 393248 | tf_op jit(solution)/shard_map/all_to_all | solution.py:355
  23.9 3.5 %gather.1 = bf16[32,544,128]{2,1,0:T(8,128)(2,1)} custom-call(s32[32,128]{1,0:T(8,128)S(1)} %bitcast.46, bf16[32,256,128]{2,1,0:T(8,128)(2,1)S(1)} %split32.1.pool_ref, bf16[32,32,128]{2,1,0:T(8,128)(2,1)S(1)} %slice.25.held_ref), custom_call_target="tpu_custom_call" | custom-call | tf_op jit(solution)/shard_map/gather/pallas_call | solution.py:116
  27.4 0.0 copy-start.1
  27.5 0.0 copy-start.3
  27.5 6.8 %all-to-all-start.1 = ((bf16[32,544,128]{2,1,0:T(8,128)(2,1)}), bf16[32,544,128]{2,1,0:T(8,128)(2,1)}, u32[]{:S(2)}, u32[]{:S(2)}) async-start(bf16[32,544,128]{2,1,0:T(8,128)(2,1)} %gather.1), calls=%async_computation.1 | async-start | bytes 8912896 | tf_op jit(solution)/shard_map/all_to_all | solution.py:355
  34.2 0.0 copy-start.2
  34.2 0.1 collective-permute-start.1
  34.4 0.0 copy-done.1
  34.5 1.5 copy_pool.1.kept_ref
  36.6 0.0 copy-done.3
  36.6 0.3 split4.1.new_ref
  36.9 0.1 add_bitcast_fusion
  37.0 0.1 add_bitcast_fusion.2
  37.1 54.4 %all-to-all-done.1.kv_any = bf16[32,544,128]{2,1,0:T(8,128)(2,1)} async-done(((bf16[32,544,128]{2,1,0:T(8,128)(2,1)}), bf16[32,544,128]{2,1,0:T(8,128)(2,1)}, u32[]{:S(2)}, u32[]{:S(2)}) %all-to-all-start.1) | async-done | bytes 4456480 | tf_op jit(solution)/shard_map/all_to_all | solution.py:355
  91.5 0.0 copy-done.2
  91.5 10.3 %attend0.1 = (bf16[64,512]{1,0:T(8,128)(2,1)S(1)}, bf16[64,512]{1,0:T(8,128)(2,1)S(1)}) custom-call(s32[1,64]{1,0:T(1,128)S(1)} %get-tuple-element.40.order, s32[1]{0:T(128)S(6)} %copy.21.length, s32[4,4]{1,0:T(4,128)S(1)} %pad_add_fusion.base, bf16[512,512]{1,0:T(8,128)(2,1)S(1)} %copy-done.2, bf16[4,256,128]{2,1,0:T(8,128)(2,1)S(1)} %split4.1.new_ref, ...), custom_call_target="tpu_custom_call" | custom-call | tf_op jit(solution)/shard_map/attend0/pallas_call | solution.py:227
  101.9 0.1 collective-permute-start
  102.0 0.0 collective-permute-done.1.refs_1_.refs_3_
  102.0 1.2 collective-permute-done.b_ref
  103.2 5.2 %project0.3 = (bf16[32,5120]{1,0:T(8,128)(2,1)S(1)}, bf16[32,5120]{1,0:T(8,128)(2,1)}) custom-call(bf16[64,512]{1,0:T(8,128)(2,1)S(1)} %get-tuple-element.27.a_ref, bf16[64,512]{1,0:T(8,128)(2,1)S(1)} %collective-permute-done.b_ref, bf16[512,5120]{1,0:T(8,128)(2,1)} %refs_2_.1, bf16[512,5120]{1,0:T(8,128)(2,1)} %collective-permute-done.1.refs_1_.refs_3_), custom_call_target="tpu_custom_call" | custom-call | tf_op jit(solution)/shard_map/project0/pallas_call | solution.py:277
  108.5 5.5 %collective-permute-start.8 = (bf16[32,5120]{1,0:T(8,128)(2,1)}, bf16[32,5120]{1,0:T(8,128)(2,1)S(1)}, u32[]{:S(2)}, u32[]{:S(2)}) collective-permute-start(bf16[32,5120]{1,0:T(8,128)(2,1)} %get-tuple-element.43), channel_id=1, source_target_pairs={{2,0},{3,1},{4,2},{5,3},{6,4},{7,5},{0,6},{1,7},{10,8},{11,9},{12,... | collective-permute-start | bytes 983048 | tf_op jit(solution)/shard_map/ppermute | solution.py:408
  113.9 0.0 collective-permute-start.7
  113.9 10.5 %attend1.1 = (bf16[64,512]{1,0:T(8,128)(2,1)S(1)}, bf16[64,512]{1,0:T(8,128)(2,1)S(1)}) custom-call(s32[1,64]{1,0:T(1,128)S(1)} %get-tuple-element.40.order, s32[1]{0:T(128)S(6)} %copy.21.length, s32[4,4]{1,0:T(4,128)S(1)} %pad_add_fusion.base, bf16[512,512]{1,0:T(8,128)(2,1)S(1)} %copy-done.2, bf16[4,256,128]{2,1,0:T(8,128)(2,1)S(1)} %split4.1.new_ref, ...), custom_call_target="tpu_custom_call" | custom-call | tf_op jit(solution)/shard_map/attend1/pallas_call | solution.py:227
  124.5 0.1 collective-permute-start.2
  124.6 1.2 collective-permute-done.2.b_ref
  125.8 5.2 %project0.4 = (bf16[32,5120]{1,0:T(8,128)(2,1)S(1)}, bf16[32,5120]{1,0:T(8,128)(2,1)}) custom-call(bf16[64,512]{1,0:T(8,128)(2,1)S(1)} %get-tuple-element.31.a_ref, bf16[64,512]{1,0:T(8,128)(2,1)S(1)} %collective-permute-done.2.b_ref, bf16[512,5120]{1,0:T(8,128)(2,1)} %refs_2_.1, bf16[512,5120]{1,0:T(8,128)(2,1)} %collective-permute-done.1.refs_1_.refs_3_), custom_call_target="tpu_custom_call" | custom-call | tf_op jit(solution)/shard_map/project0/pallas_call | solution.py:277
  131.1 4.2 %collective-permute-start.4 = (bf16[32,5120]{1,0:T(8,128)(2,1)}, bf16[32,5120]{1,0:T(8,128)(2,1)S(1)}, u32[]{:S(2)}, u32[]{:S(2)}) collective-permute-start(bf16[32,5120]{1,0:T(8,128)(2,1)} %get-tuple-element.34), channel_id=1, source_target_pairs={{2,0},{3,1},{4,2},{5,3},{6,4},{7,5},{0,6},{1,7},{10,8},{11,9},{12,... | collective-permute-start | bytes 983048 | tf_op jit(solution)/shard_map/ppermute | solution.py:410
  135.3 0.0 collective-permute-start.3
  135.3 10.3 %attend2.1 = (bf16[64,512]{1,0:T(8,128)(2,1)S(1)}, bf16[64,512]{1,0:T(8,128)(2,1)S(1)}) custom-call(s32[1,64]{1,0:T(1,128)S(1)} %get-tuple-element.40.order, s32[1]{0:T(128)S(6)} %copy.21.length, s32[4,4]{1,0:T(4,128)S(1)} %pad_add_fusion.base, bf16[512,512]{1,0:T(8,128)(2,1)S(1)} %copy-done.2, bf16[4,256,128]{2,1,0:T(8,128)(2,1)S(1)} %split4.1.new_ref, ...), custom_call_target="tpu_custom_call" | custom-call | tf_op jit(solution)/shard_map/attend2/pallas_call | solution.py:227
  145.6 0.1 collective-permute-start.6
  145.7 0.2 fusion.2
  145.9 1.1 collective-permute-done.6.b_ref
  147.0 0.0 collective-permute-done.8.refs_1_
  147.0 0.0 collective-permute-done.7.refs_0_
  147.0 4.5 %project2.1 = (bf16[32,5120]{1,0:T(8,128)(2,1)S(1)}, bf16[32,5120]{1,0:T(8,128)(2,1)S(1)}) custom-call(bf16[64,512]{1,0:T(8,128)(2,1)S(1)} %get-tuple-element.41.a_ref, bf16[64,512]{1,0:T(8,128)(2,1)S(1)} %collective-permute-done.6.b_ref, bf16[32,5120]{1,0:T(8,128)(2,1)S(1)} %collective-permute-done.7.refs_0_, ...), custom_call_target="tpu_custom_call" | custom-call | tf_op jit(solution)/shard_map/project2/pallas_call | solution.py:277
  151.5 2.1 %collective-permute-start.9 = (bf16[32,5120]{1,0:T(8,128)(2,1)S(1)}, bf16[32,5120]{1,0:T(8,128)(2,1)S(1)}, u32[]{:S(2)}, u32[]{:S(2)}) collective-permute-start(bf16[32,5120]{1,0:T(8,128)(2,1)S(1)} %get-tuple-element.44), channel_id=1, source_target_pairs={{0,2},{1,3},{2,4},{3,5},{4,6},{5,7},{6,0},{7,1},{8,10},{9,11},{10,... | collective-permute-start | bytes 983048 | tf_op jit(solution)/shard_map/ppermute | solution.py:412
  153.6 2.2 %collective-permute-start.10 = (bf16[32,5120]{1,0:T(8,128)(2,1)S(1)}, bf16[32,5120]{1,0:T(8,128)(2,1)S(1)}, u32[]{:S(2)}, u32[]{:S(2)}) collective-permute-start(bf16[32,5120]{1,0:T(8,128)(2,1)S(1)} %get-tuple-element.45), channel_id=1, source_target_pairs={{2,0},{3,1},{4,2},{5,3},{6,4},{7,5},{0,6},{1,7},{10,8},{11,9},{12,... | collective-permute-start | bytes 983048 | tf_op jit(solution)/shard_map/ppermute | solution.py:412
  155.8 0.1 fusion.slots
  155.9 0.0 collective-permute-done.4.near_down
  155.9 0.0 collective-permute-done.3.near_up
  155.9 10.5 %attend3.1 = (bf16[64,512]{1,0:T(8,128)(2,1)S(1)}, bf16[64,512]{1,0:T(8,128)(2,1)S(1)}) custom-call(s32[1,64]{1,0:T(1,128)S(1)} %get-tuple-element.40.order, s32[1]{0:T(128)S(6)} %copy.21.length, s32[4,4]{1,0:T(4,128)S(1)} %pad_add_fusion.base, bf16[512,512]{1,0:T(8,128)(2,1)S(1)} %copy-done.2, bf16[4,256,128]{2,1,0:T(8,128)(2,1)S(1)} %split4.1.new_ref, ...), custom_call_target="tpu_custom_call" | custom-call | tf_op jit(solution)/shard_map/attend3/pallas_call | solution.py:227
  166.5 0.1 collective-permute-start.5
  166.6 1.0 copy_bitcast_fusion.fresh_ref
  167.6 1.8 %write.1 = bf16[32,256,128]{2,1,0:T(8,128)(2,1)} custom-call(s32[4]{0:T(128)S(1)} %fusion.slots, bf16[4,256,128]{2,1,0:T(8,128)(2,1)S(1)} %copy_bitcast_fusion.fresh_ref, bf16[32,256,128]{2,1,0:T(8,128)(2,1)} %copy_pool.1.kept_ref), custom_call_target="tpu_custom_call", output_to_operand_aliasing={{}: (2, {})} | custom-call | tf_op jit(solution)/shard_map/write/pallas_call | solution.py:342
  169.4 0.0 collective-permute-done.5.b_ref
  169.4 4.5 %project0.5 = (bf16[32,5120]{1,0:T(8,128)(2,1)S(1)}, bf16[32,5120]{1,0:T(8,128)(2,1)S(1)}) custom-call(bf16[64,512]{1,0:T(8,128)(2,1)S(1)} %get-tuple-element.36.a_ref, bf16[64,512]{1,0:T(8,128)(2,1)S(1)} %collective-permute-done.5.b_ref, bf16[512,5120]{1,0:T(8,128)(2,1)} %refs_2_.1, bf16[512,5120]{1,0:T(8,128)(2,1)} %collective-permute-done.1.refs_1_.refs_3_), custom_call_target="tpu_custom_call" | custom-call | tf_op jit(solution)/shard_map/project0/pallas_call | solution.py:277
  174.0 0.0 collective-permute-done.9.far_up
  174.0 0.0 collective-permute-done.10.far_down
  174.0 1.1 combine.1
  (3 shorter events, 0.0 us)
Async XLA Ops:
  2.3 0.7 copy-start.4
  2.9 0.7 copy-start.5
  3.6 0.7 copy-start.6
  4.2 0.7 copy-start.7
  6.5 17.4 %all-to-all-start = ((bf16[32,48,128]{2,1,0:T(8,128)(2,1)}), bf16[32,48,128]{2,1,0:T(8,128)(2,1)S(1)}, u32[]{:S(2)}, u32[]{:S(2)}) async-start(bf16[32,48,128]{2,1,0:T(8,128)(2,1)} %get-tuple-element.26), calls=%async_computation | async-start | bytes 786432 | tf_op jit(solution)/shard_map/all_to_all | solution.py:355
  15.4 1.6 copy-start
  27.4 7.0 %copy-start.1 = (bf16[32,128,2,128]{3,2,1,0:T(2,128)(2,1)S(1)}, bf16[32,128,2,128]{3,2,1,0:T(2,128)(2,1)}, u32[]{:S(2)}) copy-start(bf16[32,128,2,128]{3,2,1,0:T(2,128)(2,1)} %param.12) | copy-start | bytes 6291460
  27.5 9.1 %copy-start.3 = (bf16[512,2,128]{2,1,0:T(2,128)(2,1)S(1)}, bf16[512,2,128]{2,1,0:T(2,128)(2,1)}, u32[]{:S(2)}) copy-start(bf16[512,2,128]{2,1,0:T(2,128)(2,1)} %param.11) | copy-start | bytes 786436
  27.5 64.1 %all-to-all-start.1 = ((bf16[32,544,128]{2,1,0:T(8,128)(2,1)}), bf16[32,544,128]{2,1,0:T(8,128)(2,1)}, u32[]{:S(2)}, u32[]{:S(2)}) async-start(bf16[32,544,128]{2,1,0:T(8,128)(2,1)} %gather.1), calls=%async_computation.1 | async-start | bytes 8912896 | tf_op jit(solution)/shard_map/all_to_all | solution.py:355
  34.2 57.3 %copy-start.2 = (bf16[512,512]{1,0:T(8,128)(2,1)S(1)}, bf16[512,512]{1,0:T(8,128)(2,1)}, u32[]{:S(2)}) copy-start(bf16[512,512]{1,0:T(8,128)(2,1)} %q_ref.7) | copy-start | bytes 1572868
  34.2 67.7 %collective-permute-start.1 = (bf16[512,5120]{1,0:T(8,128)(2,1)}, bf16[512,5120]{1,0:T(8,128)(2,1)}, u32[]{:S(2)}, u32[]{:S(2)}) collective-permute-start(bf16[512,5120]{1,0:T(8,128)(2,1)} %refs_2_.1), channel_id=1, source_target_pairs={{0,1},{1,0},{2,3},{3,2},{4,5},{5,4},{6,7},{7,6},{8,9},{9,8},{10,11... | collective-permute-start | bytes 15728648 | tf_op jit(solution)/shard_map/ppermute | solution.py:399
  101.9 1.3 collective-permute-start
  108.5 38.5 %collective-permute-start.8 = (bf16[32,5120]{1,0:T(8,128)(2,1)}, bf16[32,5120]{1,0:T(8,128)(2,1)S(1)}, u32[]{:S(2)}, u32[]{:S(2)}) collective-permute-start(bf16[32,5120]{1,0:T(8,128)(2,1)} %get-tuple-element.43), channel_id=1, source_target_pairs={{2,0},{3,1},{4,2},{5,3},{6,4},{7,5},{0,6},{1,7},{10,8},{11,9},{12,... | collective-permute-start | bytes 983048 | tf_op jit(solution)/shard_map/ppermute | solution.py:408
  113.9 33.0 %collective-permute-start.7 = (bf16[32,5120]{1,0:T(8,128)(2,1)S(1)}, bf16[32,5120]{1,0:T(8,128)(2,1)S(1)}, u32[]{:S(2)}, u32[]{:S(2)}) collective-permute-start(bf16[32,5120]{1,0:T(8,128)(2,1)S(1)} %get-tuple-element.29), channel_id=1, source_target_pairs={{0,2},{1,3},{2,4},{3,5},{4,6},{5,7},{6,0},{7,1},{8,10},{9,11},{10,... | collective-permute-start | bytes 983048 | tf_op jit(solution)/shard_map/ppermute | solution.py:408
  124.5 1.3 collective-permute-start.2
  131.1 24.9 %collective-permute-start.4 = (bf16[32,5120]{1,0:T(8,128)(2,1)}, bf16[32,5120]{1,0:T(8,128)(2,1)S(1)}, u32[]{:S(2)}, u32[]{:S(2)}) collective-permute-start(bf16[32,5120]{1,0:T(8,128)(2,1)} %get-tuple-element.34), channel_id=1, source_target_pairs={{2,0},{3,1},{4,2},{5,3},{6,4},{7,5},{0,6},{1,7},{10,8},{11,9},{12,... | collective-permute-start | bytes 983048 | tf_op jit(solution)/shard_map/ppermute | solution.py:410
  135.3 20.6 %collective-permute-start.3 = (bf16[32,5120]{1,0:T(8,128)(2,1)S(1)}, bf16[32,5120]{1,0:T(8,128)(2,1)S(1)}, u32[]{:S(2)}, u32[]{:S(2)}) collective-permute-start(bf16[32,5120]{1,0:T(8,128)(2,1)S(1)} %get-tuple-element.33), channel_id=1, source_target_pairs={{0,2},{1,3},{2,4},{3,5},{4,6},{5,7},{6,0},{7,1},{8,10},{9,11},{10,... | collective-permute-start | bytes 983048 | tf_op jit(solution)/shard_map/ppermute | solution.py:410
  145.6 1.3 collective-permute-start.6
  151.5 22.5 %collective-permute-start.9 = (bf16[32,5120]{1,0:T(8,128)(2,1)S(1)}, bf16[32,5120]{1,0:T(8,128)(2,1)S(1)}, u32[]{:S(2)}, u32[]{:S(2)}) collective-permute-start(bf16[32,5120]{1,0:T(8,128)(2,1)S(1)} %get-tuple-element.44), channel_id=1, source_target_pairs={{0,2},{1,3},{2,4},{3,5},{4,6},{5,7},{6,0},{7,1},{8,10},{9,11},{10,... | collective-permute-start | bytes 983048 | tf_op jit(solution)/shard_map/ppermute | solution.py:412
  153.6 20.4 %collective-permute-start.10 = (bf16[32,5120]{1,0:T(8,128)(2,1)S(1)}, bf16[32,5120]{1,0:T(8,128)(2,1)S(1)}, u32[]{:S(2)}, u32[]{:S(2)}) collective-permute-start(bf16[32,5120]{1,0:T(8,128)(2,1)S(1)} %get-tuple-element.45), channel_id=1, source_target_pairs={{2,0},{3,1},{4,2},{5,3},{6,4},{7,5},{0,6},{1,7},{10,8},{11,9},{12,... | collective-permute-start | bytes 983048 | tf_op jit(solution)/shard_map/ppermute | solution.py:412
  166.5 3.0 %collective-permute-start.5 = (bf16[64,512]{1,0:T(8,128)(2,1)S(1)}, bf16[64,512]{1,0:T(8,128)(2,1)S(1)}, u32[]{:S(2)}, u32[]{:S(2)}) collective-permute-start(bf16[64,512]{1,0:T(8,128)(2,1)S(1)} %get-tuple-element.37), channel_id=1, source_target_pairs={{0,1},{1,0},{2,3},{3,2},{4,5},{5,4},{6,7},{7,6},{8,9},{9,8},{10,11... | collective-permute-start | bytes 196616 | tf_op jit(solution)/shard_map/ppermute | solution.py:405
